TPU v7x, 256 devices: a whole 4x4x8 slice. The times are simulated.
256 devices in a mesh: sub: 64 (over x, z_lo, y, core), grp: 4 (over z_hi).
Axes of the slice: x: 4, y: 4, z: 8 (z_hi: 4, z_lo: 2; z = z_hi * 2 + z_lo), core: 2. Of those that a mesh axis runs over, the one named last changes fastest.
Arguments:
- basis: float32 [64, 3, 32, 4, 8, 512], P('sub', None, None, None, None, 'grp'), may hold values from -6 to 6
- material: int32 [64, 4, 8, 512], P('sub', None, None, 'grp'), may hold values from 0 to 7
- kappa_table: float32 [8], replicated, may hold values from 0.1 to 1
Outputs:
- factor: float32 [64, 32, 32], P('sub')
- panel: float32 [64, 8, 32, 32], P('sub')
All inputs are finite; a program needn't handle non-finite values.
Results may differ from a plain program's by a relative error of at most 0.0003.
Values sent between devices are 32-bit elements; how exact they have to be, the bound alone decides.
A program may use at most 192 MiB of HBM per device.

v0:
```python
import jax
import jax.numpy as jnp
from jax import lax
from jax.sharding import PartitionSpec as P

YDOMS = 4


MIXING = 0.5


def from_behind(value, axis, steps):
    count = lax.axis_size(axis)
    initial, last = (max(0, -steps), min(count, count - steps))
    return lax.ppermute(value, axis, [(source, source + steps) for source in range(initial, last)])


def stencil_entries():
    entries = []
    for step_x in (-1, 0, 1):
        for step_y in (-1, 0, 1):
            for step_z in (-1, 0, 1):
                norm_sq = step_x * step_x + step_y * step_y + step_z * step_z
                if norm_sq > 0:
                    entries.append((step_x, step_y, step_z, 0.5 ** (norm_sq - 1), norm_sq))
    return entries


def coupling_blocks(own_basis, padded_kappa, near_basis, extent_x, extent_y, layers):
    center = padded_kappa[1 : extent_x + 3, 1 : extent_y + 3, 1 : layers + 1]
    applied = jnp.zeros(
        (3, own_basis.shape[1], extent_x + 2, extent_y + 2, layers), own_basis.dtype
    )
    weight_sum = jnp.zeros((extent_x + 2, extent_y + 2, layers), own_basis.dtype)
    for step_x, step_y, step_z, weight, norm_sq in stencil_entries():
        span_x = slice(1 + step_x, extent_x + 3 + step_x)
        span_y = slice(1 + step_y, extent_y + 3 + step_y)
        span_z = slice(1 + step_z, layers + 1 + step_z)
        coupled = weight * 0.5 * (center + padded_kappa[span_x, span_y, span_z])
        shifted = own_basis[:, :, span_x, span_y, span_z]
        projected = step_x * shifted[0] + step_y * shifted[1] + step_z * shifted[2]
        mixed_basis = shifted + MIXING / norm_sq * jnp.stack(
            [step_x * projected, step_y * projected, step_z * projected]
        )
        applied = applied - coupled * mixed_basis
        weight_sum = weight_sum + coupled
    inner_x = slice(1, extent_x + 1)
    inner_y = slice(1, extent_y + 1)
    diagonal = (1.0 + MIXING) * weight_sum[inner_x, inner_y] + 0.5 * center[inner_x, inner_y]
    applied = applied.at[:, :, inner_x, inner_y].add(
        diagonal * own_basis[:, :, 2 : extent_x + 2, 2 : extent_y + 2, 1 : layers + 1]
    )
    regions_x = [slice(0, 1), slice(1, extent_x + 1), slice(extent_x + 1, extent_x + 2)]
    regions_y = [slice(0, 1), slice(1, extent_y + 1), slice(extent_y + 1, extent_y + 2)]
    blocks = []
    for region_x in regions_x:
        for region_y in regions_y:
            blocks.append(
                jnp.einsum(
                    "kixyz,kjxyz->ij",
                    applied[:, :, region_x, region_y],
                    near_basis[:, :, region_x, region_y],
                    precision=lax.Precision.HIGHEST,
                )
            )
    return jnp.stack(blocks)


def solve_blocks(lower, blocks):
    count = blocks.shape[0]
    width = blocks.shape[1]
    stacked = blocks.transpose(1, 0, 2).reshape(width, count * width)
    solved = jax.scipy.linalg.solve_triangular(lower, stacked, lower=True)
    return solved.reshape(width, count, width).transpose(1, 0, 2)


def shards(basis, material, kappa_table):
    local_basis = basis[0]
    extent_x = local_basis.shape[2]
    extent_y = local_basis.shape[3]
    layers = local_basis.shape[4]
    cells_here = material[0]
    kappa = jnp.zeros(cells_here.shape, jnp.float32)
    for which in range(kappa_table.shape[0]):
        kappa = kappa + jnp.where(cells_here == which, kappa_table[which], 0.0)
    below = from_behind(
        (local_basis[:, :, :, :, layers - 1 :], kappa[:, :, layers - 1 :]), "grp", 1
    )
    above = from_behind((local_basis[:, :, :, :, :1], kappa[:, :, :1]), "grp", -1)
    slab_basis = jnp.concatenate([below[0], local_basis, above[0]], axis=4)
    slab_kappa = jnp.concatenate([below[1], kappa, above[1]], axis=2)
    column = lax.axis_index("sub") % YDOMS
    keep_low = (column > 0).astype(jnp.float32)
    keep_high = (column < YDOMS - 1).astype(jnp.float32)
    from_low = from_behind(
        (slab_basis[:, :, :, extent_y - 1 :], slab_kappa[:, extent_y - 1 :]), "sub", 1
    )
    from_high = from_behind((slab_basis[:, :, :, :1], slab_kappa[:, :1]), "sub", -1)
    wide_basis = jnp.concatenate(
        [from_low[0] * keep_low, slab_basis, from_high[0] * keep_high], axis=3
    )
    wide_kappa = jnp.concatenate(
        [from_low[1] * keep_low, slab_kappa, from_high[1] * keep_high], axis=1
    )
    from_west = from_behind(
        (wide_basis[:, :, extent_x - 1 :], wide_kappa[extent_x - 1 :]), "sub", YDOMS
    )
    from_east = from_behind((wide_basis[:, :, :1], wide_kappa[:1]), "sub", -YDOMS)
    west_basis, west_kappa = from_west
    east_basis, east_kappa = from_east
    full_basis = jnp.concatenate([west_basis, wide_basis, east_basis], axis=2)
    full_kappa = jnp.concatenate([west_kappa, wide_kappa, east_kappa], axis=0)
    own_basis = jnp.pad(slab_basis, ((0, 0), (0, 0), (2, 2), (2, 2), (0, 0)))
    padded_kappa = jnp.pad(full_kappa, ((1, 1), (1, 1), (0, 0)))
    near_basis = full_basis[:, :, :, :, 1 : layers + 1]
    partial_value = coupling_blocks(own_basis, padded_kappa, near_basis, extent_x, extent_y, layers)
    totals = lax.psum(partial_value, "grp")
    lower = jnp.linalg.cholesky(totals[4])
    panel = solve_blocks(lower, jnp.concatenate([totals[:4], totals[5:]], axis=0))
    cell_count = 3.0 * extent_x * extent_y * layers * lax.axis_size("grp")
    return ((lower / jnp.sqrt(cell_count))[None], panel[None])


def solution(mesh):
    placed = (P("sub", None, None, None, None, "grp"), P("sub", None, None, "grp"), P())
    return jax.shard_map(
        shards,
        mesh=mesh,
        in_specs=placed,
        out_specs=(P("sub", None, None), P("sub", None, None, None)),
        check_vma=False,
    )
```

profile of v0, /device:TPU:6, one launch (start us, length us, event | category | flops | bytes accessed | tf_op | source)
XLA Modules:
  0.0 204.5 jit_solution(10115469109979025099)
XLA Ops:
  0.6 1.6 fusion.312
  2.3 5.8 %add_bitcast_fusion = f32[4,8,128]{2,1,0:T(8,128)S(1)} fusion(s32[1,4,8,128]{3,2,1,0:T(8,128)} %param.6, f32[]{:T(128)} %bitcast.7, f32[]{:T(128)} %bitcast.6, f32[]{:T(128)} %bitcast.5, f32[]{:T(128)} %bitcast.4, f32[]{:T(128)} %bitcast.3, f32[]{:T(128)} %bitcast.2, f32[]{:T(128)} %bitcast.1, f32[]{:T(128)} %bitcast), kind=kLoop, calls=%fused_computation.495 | loop fusion | flops 94208 | bytes 32800 | tf_op jit(solution)/shard_map/add | solution.py:85
  8.1 5.2 %collective-permute-start = (f32[4,8,1]{2,1,0:T(8,128)S(1)}, f32[4,8,1]{2,1,0:T(8,128)S(1)}, u32[]{:S(2)}, u32[]{:S(2)}) collective-permute-start(f32[4,8,1]{2,1,0:T(8,128)S(1)} %get-tuple-element.155), channel_id=1, source_target_pairs={{0,1},{1,2},{2,3},{4,5},{5,6},{6,7},{8,9},{9,10},{10,11},{12,13},{... | collective-permute-start | bytes 392 | tf_op jit(solution)/shard_map/ppermute | solution.py:15
  13.3 1.3 collective-permute-start.1
  14.7 6.7 %collective-permute-done.1 = f32[4,8,1]{2,1,0:T(8,128)S(1)} collective-permute-done((f32[4,8,1]{2,1,0:T(8,128)S(1)}, f32[4,8,1]{2,1,0:T(8,128)S(1)}, u32[]{:S(2)}, u32[]{:S(2)}) %collective-permute-start.1) | collective-permute-done | bytes 160 | tf_op jit(solution)/shard_map/ppermute | solution.py:15
  21.5 1.9 collective-permute-start.2
  23.4 2.3 %copy.107 = f32[1,3,32,4,8,128]{5,2,1,4,3,0:T(8,128)S(1)} copy(f32[1,3,32,4,8,128]{5,4,3,2,1,0:T(8,128)} %param.5) | data formatting | bytes 3145728 | tf_op args[0]
  25.8 6.7 %collective-permute-start.3 = (f32[4,1,130]{2,1,0:T(1,128)S(1)}, f32[4,1,130]{2,1,0:T(1,128)S(1)}, u32[]{:S(2)}, u32[]{:S(2)}) collective-permute-start(f32[4,1,130]{2,1,0:T(1,128)S(1)} %get-tuple-element.152), channel_id=1, source_target_pairs={{4,0},{8,4},{12,8},{16,12},{20,16},{24,20},{28,24},{32,28},{36,32}... | collective-permute-start | bytes 6248 | tf_op jit(solution)/shard_map/ppermute | solution.py:15
  32.4 1.3 collective-permute-done.3
  33.8 2.1 %collective-permute-start.4 = (f32[1,10,130]{2,1,0:T(8,128)S(1)}, f32[1,10,130]{2,1,0:T(8,128)S(1)}, u32[]{:S(2)}, u32[]{:S(2)}) collective-permute-start(f32[1,10,130]{2,1,0:T(8,128)S(1)} %get-tuple-element.149), channel_id=1, source_target_pairs={{0,16},{4,20},{8,24},{12,28},{16,32},{20,36},{24,40},{28,44},{32,4... | collective-permute-start | bytes 15608 | tf_op jit(solution)/shard_map/ppermute | solution.py:15
  35.9 7.1 %collective-permute-start.5 = (f32[1,10,130]{2,1,0:T(8,128)S(1)}, f32[1,10,130]{2,1,0:T(8,128)S(1)}, u32[]{:S(2)}, u32[]{:S(2)}) collective-permute-start(f32[1,10,130]{2,1,0:T(8,128)S(1)} %get-tuple-element.150), channel_id=1, source_target_pairs={{16,0},{20,4},{24,8},{28,12},{32,16},{36,20},{40,24},{44,28},{48,3... | collective-permute-start | bytes 15608 | tf_op jit(solution)/shard_map/ppermute | solution.py:15
  44.2 1.3 collective-permute-start.7
  46.1 6.7 %collective-permute-start.6 = (f32[3,32,4,8,1]{1,3,4,2,0:T(8,128)S(1)}, f32[3,32,4,8,1]{1,3,4,2,0:T(8,128)S(1)}, u32[]{:S(2)}, u32[]{:S(2)}) collective-permute-start(f32[3,32,4,8,1]{1,3,4,2,0:T(8,128)S(1)} %copy.28), channel_id=1, source_target_pairs={{0,1},{1,2},{2,3},{4,5},{5,6},{6,7},{8,9},{9,10},{10,11},{12,13},{... | collective-permute-start | bytes 36872 | tf_op jit(solution)/shard_map/ppermute | solution.py:15
  53.1 1.2 add_add_fusion
  54.3 5.1 %fusion.260 = f32[4,8,128]{2,1,0:T(8,128)S(1)} fusion(f32[6,10,128]{2,1,0:T(8,128)S(1)} %get-tuple-element.146, f32[6,10,128]{2,1,0:T(8,128)S(1)} %get-tuple-element.145, f32[6,10,128]{2,1,0:T(8,128)S(1)} %get-tuple-element.144, f32[6,10,128]{2,1,0:T(8,128)S(1)} %get-tuple-element.147, f32[6,10,128]{2,1,0:T(8,128)S(1)} %get-tuple-element.148, ...), kind=kLoop, calls=%fused_computation.481 | loop fusion | flops 131072 | bytes 147488 | tf_op jit(solution)/shard_map/add | solution.py:49
  59.4 1.8 copy.30
  61.2 1.9 copy.31
  63.1 3.6 %pad_maximum_fusion = f32[3,32,4,8,130]{4,1,0,3,2:T(8,128)S(1)} fusion(f32[3,32,4,8,1]{4,1,0,3,2:T(8,128)} %copy.31, f32[3,32,4,8,128]{4,1,0,3,2:T(8,128)} %bitcast.152, f32[3,32,4,8,1]{4,1,0,3,2:T(8,128)} %copy.30), kind=kLoop, calls=%fused_computation.104 | loop fusion | flops 798720 | bytes 3194880 | tf_op jit(solution)/shard_map/concatenate | solution.py:90
  66.7 0.8 fusion.308
  67.6 6.5 %broadcast_multiply_fusion.29 = (f32[1,32,6,10,128]{4,1,0,3,2:T(8,128)}, f32[1,32,6,10,128]{4,1,0,3,2:T(8,128)}, f32[1,32,6,10,128]{4,1,0,3,2:T(8,128)}, f32[1,3...) fusion(f32[3,32,4,8,130]{4,1,0,3,2:T(8,128)S(1)} %pad_maximum_f, ...), kind=kLoop, calls=%fused_computation.365 | loop fusion | flops 8355840 | bytes 15360000 | tf_op jit(solution)/shard_map/mul | solution.py:43
  74.0 13.7 %broadcast_multiply_fusion.35 = (f32[1,32,6,10,128]{4,1,0,3,2:T(8,128)}, f32[1,32,6,10,128]{4,1,0,3,2:T(8,128)}, f32[32,6,10,128]{3,0,2,1:T(8,128)}, f32[32,6,10...) fusion(f32[3,32,4,8,130]{4,1,0,3,2:T(8,128)S(1)} %pad_maximum_f, ...), kind=kLoop, calls=%fused_computation.371 | loop fusion | flops 21626880 | bytes 36986880 | tf_op jit(solution)/shard_map/mul | solution.py:43
  87.7 2.1 %collective-permute-start.8 = (f32[3,32,4,1,130]{4,1,0,3,2:T(8,128)S(1)}, f32[3,32,4,1,130]{4,1,0,3,2:T(8,128)S(1)}, u32[]{:S(2)}, u32[]{:S(2)}) collective-permute-start(f32[3,32,4,1,130]{4,1,0,3,2:T(8,128)S(1)} %get-tuple-element.133), channel_id=1, source_target_pairs={{0,4},{4,8},{8,12},{12,16},{16,20},{20,24},{24,28},{28,32},{32,36}... | collective-permute-start | bytes 599048 | tf_op jit(solution)/shard_map/ppermute | solution.py:15
  89.8 6.7 %collective-permute-start.9 = (f32[3,32,4,1,130]{4,1,0,3,2:T(8,128)}, f32[3,32,4,1,130]{4,1,0,3,2:T(8,128)S(1)}, u32[]{:S(2)}, u32[]{:S(2)}) collective-permute-start(f32[3,32,4,1,130]{4,1,0,3,2:T(8,128)} %get-tuple-element.134), channel_id=1, source_target_pairs={{4,0},{8,4},{12,8},{16,12},{20,16},{24,20},{28,24},{32,28},{36,32}... | collective-permute-start | bytes 599048 | tf_op jit(solution)/shard_map/ppermute | solution.py:15
  96.5 3.0 %broadcast_multiply_fusion.10 = (f32[1,32,6,10,128]{4,1,0,3,2:T(8,128)}, f32[1,32,6,10,128]{4,1,0,3,2:T(8,128)}) fusion(f32[1,32,6,10,128]{4,1,0,3,2:T(8,128)} %get-tuple-element.124, f32[1,32,6,10,128]{4,1,0,3,2:T(8,128)} %get-tuple-element.128), kind=kLoop, calls=%fused_computation.346 | loop fusion | flops 491520 | bytes 3932160 | tf_op jit(solution)/shard_map/mul | solution.py:43
  99.5 1.5 broadcast_multiply_fusion.21
  101.0 0.7 copy-done.14
  101.7 1.5 broadcast_multiply_fusion.14
  103.2 1.5 broadcast_multiply_fusion.26
  105.4 1.5 broadcast_multiply_fusion.23
  107.0 1.5 broadcast_multiply_fusion.1
  110.0 2.0 pad_maximum_fusion.1
  112.0 2.1 %collective-permute-start.10 = (f32[3,32,1,10,130]{4,1,0,3,2:T(8,128)}, f32[3,32,1,10,130]{4,1,0,3,2:T(8,128)}, u32[]{:S(2)}, u32[]{:S(2)}) collective-permute-start(f32[3,32,1,10,130]{4,1,0,3,2:T(8,128)} %get-tuple-element.84), channel_id=1, source_target_pairs={{0,16},{4,20},{8,24},{12,28},{16,32},{20,36},{24,40},{28,44},{32,4... | collective-permute-start | bytes 1497608 | tf_op jit(solution)/shard_map/ppermute | solution.py:15
  114.1 29.8 %fusion.67 = f32[3,32,6,10,128]{4,1,0,3,2:T(8,128)} fusion(f32[3,32,4,8,130]{4,1,0,3,2:T(8,128)S(1)} %pad_maximum_fusion, f32[1,32,6,10,128]{4,1,0,3,2:T(8,128)} %get-tuple-element.171, f32[1,32,6,10,128]{4,1,0,3,2:T(8,128)} %get-tuple-element.91, f32[1,32,6,10,128]{4,1,0,3,2:T(8,128)} %get-tuple-element.92, f32[1,32,6,10,128]{4,1,0,3,2:T(8,128)} %get-tuple-element.97, ...), kind=kLoop, calls=%fused_computation.172 | loop fusion | flops 110592000 | bytes 60395520 | tf_op jit(solution)/shard_map/sub | solution.py:45
  143.9 1.2 slice_bitcast_fusion.5
  145.1 1.2 slice_bitcast_fusion.1
  146.3 7.2 %collective-permute-start.11 = (f32[3,32,1,10,130]{4,1,0,3,2:T(8,128)}, f32[3,32,1,10,130]{4,1,0,3,2:T(8,128)S(1)}, u32[]{:S(2)}, u32[]{:S(2)}) collective-permute-start(f32[3,32,1,10,130]{4,1,0,3,2:T(8,128)} %get-tuple-element.83), channel_id=1, source_target_pairs={{16,0},{20,4},{24,8},{28,12},{32,16},{36,20},{40,24},{44,28},{48,3... | collective-permute-start | bytes 1497608 | tf_op jit(solution)/shard_map/ppermute | solution.py:15
  153.5 1.2 fusion.96
  154.7 1.7 fusion.95
  156.3 1.2 fusion.94
  157.9 4.5 %fusion.86 = f32[9,32,32]{1,2,0:T(8,128)S(1)} fusion(f32[9,32,32]{1,2,0:T(8,128)S(1)} %fusion.98, f32[3,32,4,8,128]{4,3,2,1,0:T(8,128)S(1)} %bitcast.154, f32[3,32,6,10,128]{4,1,0,3,2:T(8,128)} %fusion.67, f32[4,8,128]{2,1,0:T(8,128)S(1)} %fusion.260, f32[1,3,32,4,8,128]{5,4,3,2,1,0:T(8,128)S(1)} %copy-done.2), kind=kOutput, calls=%fused_computation.214 | convolution fusion | flops 151781376 | bytes 4751360 | tf_op jit(solution)/shard_map/kixyz,kjxyz->ij/dot_general | solution.py:59
  162.8 7.6 %collective-permute-done.11 = f32[3,32,1,10,130]{4,1,0,3,2:T(8,128)S(1)} collective-permute-done((f32[3,32,1,10,130]{4,1,0,3,2:T(8,128)}, f32[3,32,1,10,130]{4,1,0,3,2:T(8,128)S(1)}, u32[]{:S(2)}, u32[]{:S(2)}) %collective-permute-start.11) | collective-permute-done | bytes 499232 | tf_op jit(solution)/shard_map/ppermute | solution.py:15
  170.5 1.0 fusion.93
  172.0 1.0 fusion.91
  173.1 22.6 %psum.7 = f32[9,32,32]{1,2,0:T(8,128)S(1)} all-reduce(f32[9,32,32]{1,2,0:T(8,128)S(1)} %fusion.91), channel_id=1, replica_groups=mesh['sub'=64,'grp'=4] {'grp'}, use_global_device_ids=true, to_apply=%region_0.1 | all-reduce | flops 9216 | bytes 73728 | tf_op jit(solution)/shard_map/psum | solution.py:117
  195.8 2.9 %cholesky.18 = f32[32,32]{1,0:T(8,128)S(1)} custom-call(f32[32,32]{1,0:T(8,128)S(1)} %fusion.262), custom_call_target="Cholesky" | custom-call | tf_op jit(solution)/shard_map/jit(cholesky)/cholesky | solution.py:118
  199.4 1.3 select_bitcast_fusion
  200.6 2.4 %custom-call.7 = f32[1,32,32]{1,2,0:T(8,128)S(1)} custom-call(f32[1,32,32]{2,1,0:T(8,128)S(1)} %get-tuple-element.153), custom_call_target="InvertDiagBlocksLowerTriangular" | custom-call | tf_op jit(solution)/shard_map/jit(_solve_triangular)/triangular_solve | solution.py:73
  203.1 1.4 convolution_bitcast_fusion
  (81 shorter events, 6.7 us)
Async XLA Ops:
  8.1 6.6 %collective-permute-start = (f32[4,8,1]{2,1,0:T(8,128)S(1)}, f32[4,8,1]{2,1,0:T(8,128)S(1)}, u32[]{:S(2)}, u32[]{:S(2)}) collective-permute-start(f32[4,8,1]{2,1,0:T(8,128)S(1)} %get-tuple-element.155), channel_id=1, source_target_pairs={{0,1},{1,2},{2,3},{4,5},{5,6},{6,7},{8,9},{9,10},{10,11},{12,13},{... | collective-permute-start | bytes 392 | tf_op jit(solution)/shard_map/ppermute | solution.py:15
  13.3 8.1 %collective-permute-start.1 = (f32[4,8,1]{2,1,0:T(8,128)S(1)}, f32[4,8,1]{2,1,0:T(8,128)S(1)}, u32[]{:S(2)}, u32[]{:S(2)}) collective-permute-start(f32[4,8,1]{2,1,0:T(8,128)S(1)} %get-tuple-element.156), channel_id=1, source_target_pairs={{1,0},{2,1},{3,2},{5,4},{6,5},{7,6},{9,8},{10,9},{11,10},{13,12},{... | collective-permute-start | bytes 392 | tf_op jit(solution)/shard_map/ppermute | solution.py:15
  21.5 10.9 %collective-permute-start.2 = (f32[4,1,130]{2,1,0:T(1,128)S(1)}, f32[4,1,130]{2,1,0:T(1,128)S(1)}, u32[]{:S(2)}, u32[]{:S(2)}) collective-permute-start(f32[4,1,130]{2,1,0:T(1,128)S(1)} %get-tuple-element.151), channel_id=1, source_target_pairs={{0,4},{4,8},{8,12},{12,16},{16,20},{20,24},{24,28},{28,32},{32,36}... | collective-permute-start | bytes 6248 | tf_op jit(solution)/shard_map/ppermute | solution.py:15
  25.7 17.8 %copy-start = (f32[1,3,32,4,8,128]{5,2,1,4,3,0:T(8,128)}, f32[1,3,32,4,8,128]{5,2,1,4,3,0:T(8,128)S(1)}, u32[]{:S(2)}) copy-start(f32[1,3,32,4,8,128]{5,2,1,4,3,0:T(8,128)S(1)} %copy.107) | copy-start | bytes 4718596
  25.8 8.0 %collective-permute-start.3 = (f32[4,1,130]{2,1,0:T(1,128)S(1)}, f32[4,1,130]{2,1,0:T(1,128)S(1)}, u32[]{:S(2)}, u32[]{:S(2)}) collective-permute-start(f32[4,1,130]{2,1,0:T(1,128)S(1)} %get-tuple-element.152), channel_id=1, source_target_pairs={{4,0},{8,4},{12,8},{16,12},{20,16},{24,20},{28,24},{32,28},{36,32}... | collective-permute-start | bytes 6248 | tf_op jit(solution)/shard_map/ppermute | solution.py:15
  33.8 19.0 %collective-permute-start.4 = (f32[1,10,130]{2,1,0:T(8,128)S(1)}, f32[1,10,130]{2,1,0:T(8,128)S(1)}, u32[]{:S(2)}, u32[]{:S(2)}) collective-permute-start(f32[1,10,130]{2,1,0:T(8,128)S(1)} %get-tuple-element.149), channel_id=1, source_target_pairs={{0,16},{4,20},{8,24},{12,28},{16,32},{20,36},{24,40},{28,44},{32,4... | collective-permute-start | bytes 15608 | tf_op jit(solution)/shard_map/ppermute | solution.py:15
  35.9 16.9 %collective-permute-start.5 = (f32[1,10,130]{2,1,0:T(8,128)S(1)}, f32[1,10,130]{2,1,0:T(8,128)S(1)}, u32[]{:S(2)}, u32[]{:S(2)}) collective-permute-start(f32[1,10,130]{2,1,0:T(8,128)S(1)} %get-tuple-element.150), channel_id=1, source_target_pairs={{16,0},{20,4},{24,8},{28,12},{32,16},{36,20},{40,24},{44,28},{48,3... | collective-permute-start | bytes 15608 | tf_op jit(solution)/shard_map/ppermute | solution.py:15
  43.5 10.7 %copy-start.25 = (s32[1,4,8,128]{3,2,1,0:T(8,128)S(1)}, s32[1,4,8,128]{3,2,1,0:T(8,128)}, u32[]{:S(2)}) copy-start(s32[1,4,8,128]{3,2,1,0:T(8,128)} %param.6) | copy-start | bytes 49156
  44.2 17.1 %collective-permute-start.7 = (f32[3,32,4,8,1]{1,3,4,2,0:T(8,128)S(1)}, f32[3,32,4,8,1]{1,3,4,2,0:T(8,128)S(1)}, u32[]{:S(2)}, u32[]{:S(2)}) collective-permute-start(f32[3,32,4,8,1]{1,3,4,2,0:T(8,128)S(1)} %copy.29), channel_id=1, source_target_pairs={{1,0},{2,1},{3,2},{5,4},{6,5},{7,6},{9,8},{10,9},{11,10},{13,12},{... | collective-permute-start | bytes 36872 | tf_op jit(solution)/shard_map/ppermute | solution.py:15
  46.1 13.3 %collective-permute-start.6 = (f32[3,32,4,8,1]{1,3,4,2,0:T(8,128)S(1)}, f32[3,32,4,8,1]{1,3,4,2,0:T(8,128)S(1)}, u32[]{:S(2)}, u32[]{:S(2)}) collective-permute-start(f32[3,32,4,8,1]{1,3,4,2,0:T(8,128)S(1)} %copy.28), channel_id=1, source_target_pairs={{0,1},{1,2},{2,3},{4,5},{5,6},{6,7},{8,9},{9,10},{10,11},{12,13},{... | collective-permute-start | bytes 36872 | tf_op jit(solution)/shard_map/ppermute | solution.py:15
  53.0 1.3 copy-start.15
  53.0 6.3 %copy-start.17 = (f32[6,10,128]{2,1,0:T(8,128)}, f32[6,10,128]{2,1,0:T(8,128)S(1)}, u32[]{:S(2)}) copy-start(f32[6,10,128]{2,1,0:T(8,128)S(1)} %get-tuple-element.144) | copy-start | bytes 92164
  53.0 6.3 %copy-start.19 = (f32[6,10,128]{2,1,0:T(8,128)}, f32[6,10,128]{2,1,0:T(8,128)S(1)}, u32[]{:S(2)}) copy-start(f32[6,10,128]{2,1,0:T(8,128)S(1)} %get-tuple-element.145) | copy-start | bytes 92164
  53.0 6.3 %copy-start.21 = (f32[6,10,128]{2,1,0:T(8,128)}, f32[6,10,128]{2,1,0:T(8,128)S(1)}, u32[]{:S(2)}) copy-start(f32[6,10,128]{2,1,0:T(8,128)S(1)} %get-tuple-element.146) | copy-start | bytes 92164
  53.1 6.3 %copy-start.23 = (f32[6,10,128]{2,1,0:T(8,128)}, f32[6,10,128]{2,1,0:T(8,128)S(1)}, u32[]{:S(2)}) copy-start(f32[6,10,128]{2,1,0:T(8,128)S(1)} %get-tuple-element.147) | copy-start | bytes 92164
  53.1 6.3 %copy-start.24 = (f32[6,10,128]{2,1,0:T(8,128)}, f32[6,10,128]{2,1,0:T(8,128)S(1)}, u32[]{:S(2)}) copy-start(f32[6,10,128]{2,1,0:T(8,128)S(1)} %get-tuple-element.148) | copy-start | bytes 92164
  87.7 11.8 %copy-start.5 = (f32[1,32,6,10,128]{4,1,0,3,2:T(8,128)S(1)}, f32[1,32,6,10,128]{4,1,0,3,2:T(8,128)}, u32[]{:S(2)}) copy-start(f32[1,32,6,10,128]{4,1,0,3,2:T(8,128)} %get-tuple-element.126) | copy-start | bytes 2949124
  87.7 11.8 %copy-start.10 = (f32[1,32,6,10,128]{4,1,0,3,2:T(8,128)S(1)}, f32[1,32,6,10,128]{4,1,0,3,2:T(8,128)}, u32[]{:S(2)}) copy-start(f32[1,32,6,10,128]{4,1,0,3,2:T(8,128)} %get-tuple-element.130) | copy-start | bytes 2949124
  87.7 20.8 %collective-permute-start.8 = (f32[3,32,4,1,130]{4,1,0,3,2:T(8,128)S(1)}, f32[3,32,4,1,130]{4,1,0,3,2:T(8,128)S(1)}, u32[]{:S(2)}, u32[]{:S(2)}) collective-permute-start(f32[3,32,4,1,130]{4,1,0,3,2:T(8,128)S(1)} %get-tuple-element.133), channel_id=1, source_target_pairs={{0,4},{4,8},{8,12},{12,16},{16,20},{20,24},{24,28},{28,32},{32,36}... | collective-permute-start | bytes 599048 | tf_op jit(solution)/shard_map/ppermute | solution.py:15
  89.8 18.8 %collective-permute-start.9 = (f32[3,32,4,1,130]{4,1,0,3,2:T(8,128)}, f32[3,32,4,1,130]{4,1,0,3,2:T(8,128)S(1)}, u32[]{:S(2)}, u32[]{:S(2)}) collective-permute-start(f32[3,32,4,1,130]{4,1,0,3,2:T(8,128)} %get-tuple-element.134), channel_id=1, source_target_pairs={{4,0},{8,4},{12,8},{16,12},{20,16},{24,20},{28,24},{32,28},{36,32}... | collective-permute-start | bytes 599048 | tf_op jit(solution)/shard_map/ppermute | solution.py:15
  99.5 1.5 copy-start.13
  99.5 2.2 %copy-start.14 = (f32[1,32,6,10,128]{4,1,0,3,2:T(8,128)S(1)}, f32[1,32,6,10,128]{4,1,0,3,2:T(8,128)}, u32[]{:S(2)}) copy-start(f32[1,32,6,10,128]{4,1,0,3,2:T(8,128)} %get-tuple-element.100) | copy-start | bytes 2949124
  101.0 2.2 %copy-start.6 = (f32[1,32,6,10,128]{4,1,0,3,2:T(8,128)S(1)}, f32[1,32,6,10,128]{4,1,0,3,2:T(8,128)}, u32[]{:S(2)}) copy-start(f32[1,32,6,10,128]{4,1,0,3,2:T(8,128)} %get-tuple-element.92) | copy-start | bytes 2949124
  101.0 2.2 %copy-start.12 = (f32[1,32,6,10,128]{4,1,0,3,2:T(8,128)S(1)}, f32[1,32,6,10,128]{4,1,0,3,2:T(8,128)}, u32[]{:S(2)}) copy-start(f32[1,32,6,10,128]{4,1,0,3,2:T(8,128)} %get-tuple-element.94) | copy-start | bytes 2949124
  103.2 1.5 copy-start.8
  103.2 2.2 %copy-start.11 = (f32[1,32,6,10,128]{4,1,0,3,2:T(8,128)S(1)}, f32[1,32,6,10,128]{4,1,0,3,2:T(8,128)}, u32[]{:S(2)}) copy-start(f32[1,32,6,10,128]{4,1,0,3,2:T(8,128)} %get-tuple-element.120) | copy-start | bytes 2949124
  104.7 2.2 %copy-start.7 = (f32[1,32,6,10,128]{4,1,0,3,2:T(8,128)S(1)}, f32[1,32,6,10,128]{4,1,0,3,2:T(8,128)}, u32[]{:S(2)}) copy-start(f32[1,32,6,10,128]{4,1,0,3,2:T(8,128)} %get-tuple-element.104) | copy-start | bytes 2949124
  104.7 2.3 %copy-start.9 = (f32[1,32,6,10,128]{4,1,0,3,2:T(8,128)S(1)}, f32[1,32,6,10,128]{4,1,0,3,2:T(8,128)}, u32[]{:S(2)}) copy-start(f32[1,32,6,10,128]{4,1,0,3,2:T(8,128)} %get-tuple-element.118) | copy-start | bytes 2949124
  106.9 1.9 copy-start.1
  106.9 2.6 %copy-start.3 = (f32[3,32,4,8,1]{4,1,0,3,2:T(8,128)S(1)}, f32[3,32,4,8,1]{4,1,0,3,2:T(8,128)}, u32[]{:S(2)}) copy-start(f32[3,32,4,8,1]{4,1,0,3,2:T(8,128)} %copy.30) | copy-start | bytes 36868
  106.9 3.1 %copy-start.4 = (f32[3,32,4,8,1]{4,1,0,3,2:T(8,128)S(1)}, f32[3,32,4,8,1]{4,1,0,3,2:T(8,128)}, u32[]{:S(2)}) copy-start(f32[3,32,4,8,1]{4,1,0,3,2:T(8,128)} %copy.31) | copy-start | bytes 36868
  110.0 4.1 %copy-start.16 = (f32[6,10,128]{2,1,0:T(8,128)S(1)}, f32[6,10,128]{2,1,0:T(8,128)}, u32[]{:S(2)}) copy-start(f32[6,10,128]{2,1,0:T(8,128)} %copy-done.15) | copy-start | bytes 92164
  110.0 4.1 %copy-start.18 = (f32[6,10,128]{2,1,0:T(8,128)S(1)}, f32[6,10,128]{2,1,0:T(8,128)}, u32[]{:S(2)}) copy-start(f32[6,10,128]{2,1,0:T(8,128)} %copy-done.17) | copy-start | bytes 92164
  110.0 4.1 %copy-start.20 = (f32[6,10,128]{2,1,0:T(8,128)S(1)}, f32[6,10,128]{2,1,0:T(8,128)}, u32[]{:S(2)}) copy-start(f32[6,10,128]{2,1,0:T(8,128)} %copy-done.19) | copy-start | bytes 92164
  110.0 4.1 %copy-start.22 = (f32[6,10,128]{2,1,0:T(8,128)S(1)}, f32[6,10,128]{2,1,0:T(8,128)}, u32[]{:S(2)}) copy-start(f32[6,10,128]{2,1,0:T(8,128)} %copy-done.21) | copy-start | bytes 92164
  112.0 41.5 %collective-permute-start.10 = (f32[3,32,1,10,130]{4,1,0,3,2:T(8,128)}, f32[3,32,1,10,130]{4,1,0,3,2:T(8,128)}, u32[]{:S(2)}, u32[]{:S(2)}) collective-permute-start(f32[3,32,1,10,130]{4,1,0,3,2:T(8,128)} %get-tuple-element.84), channel_id=1, source_target_pairs={{0,16},{4,20},{8,24},{12,28},{16,32},{20,36},{24,40},{28,44},{32,4... | collective-permute-start | bytes 1497608 | tf_op jit(solution)/shard_map/ppermute | solution.py:15
  143.9 14.0 %copy-start.2 = (f32[1,3,32,4,8,128]{5,4,3,2,1,0:T(8,128)S(1)}, f32[1,3,32,4,8,128]{5,4,3,2,1,0:T(8,128)}, u32[]{:S(2)}) copy-start(f32[1,3,32,4,8,128]{5,4,3,2,1,0:T(8,128)} %param.5) | copy-start | bytes 4718596
  146.3 24.2 %collective-permute-start.11 = (f32[3,32,1,10,130]{4,1,0,3,2:T(8,128)}, f32[3,32,1,10,130]{4,1,0,3,2:T(8,128)S(1)}, u32[]{:S(2)}, u32[]{:S(2)}) collective-permute-start(f32[3,32,1,10,130]{4,1,0,3,2:T(8,128)} %get-tuple-element.83), channel_id=1, source_target_pairs={{16,0},{20,4},{24,8},{28,12},{32,16},{36,20},{40,24},{44,28},{48,3... | collective-permute-start | bytes 1497608 | tf_op jit(solution)/shard_map/ppermute | solution.py:15
where the time goes:
time: 206 us; the launch traced here: 204 us
  other arithmetic  85.9 us (42%)
  starting transfers between devices  50.1 us (24%)
  blocking collectives  22.6 us (11%)
  waiting for transfers between devices  15.8 us (8%)
  local copies, waits for them, and re-layouts  15.7 us (8%)
  matrix products  13.3 us (6%)
    ppermute x12, starting transfers between devices, from_behind(): lax.ppermute(value, axis, [(source, source + steps) for source in range(i...  50.1 us
    sub x1, other arithmetic, coupling_blocks(): applied = applied - coupled * mixed_basis  29.8 us
    mul x3, other arithmetic, coupling_blocks(): step_x * projected  23.2 us
    psum x1, blocking collectives, shards(): totals = lax.psum(partial_value, 'grp')  22.6 us
    ppermute x12, waiting for transfers between devices, from_behind(): lax.ppermute(value, axis, [(source, source + steps) for source in range(i...  15.8 us
    dot_general x9, matrix products, coupling_blocks(): jnp.einsum('kixyz,kjxyz->ij', applied[:, :, region_x, region_y], near_bas...  11.8 us
    add x1, other arithmetic, shards(): kappa = kappa + jnp.where(cells_here == which, kappa_table[which], 0.0)  5.76 us
    unnamed x53, local copies, waits for them, and re-layouts  5.24 us
  transfers between devices with their start and end apart: 12, of which 4 were waited for; matrix products, arithmetic and copies ran while one was open for 31% of the time, Pallas kernels for 0%

commit v1 on v0

v1 whole, which is shorter than its diff:
```python
import functools

import jax
import jax.numpy as jnp
import numpy as np
from jax import lax
from jax.experimental import pallas as pl
from jax.experimental.pallas import tpu as pltpu
from jax.sharding import PartitionSpec as P

YDOMS = 4
XDOMS = 16
SLABS = 4
MESH = pl.DeviceIdType.MESH
F32 = jnp.float32
BF16 = jnp.bfloat16
GHOSTS = 42
ROWS = 144
ALL_NEAR = [(p, r) for p in (-1, 0, 1) for r in (-1, 0, 1) if (p, r) != (0, 0)]
FORWARD = [(0, 1), (1, -1), (1, 0), (1, 1)]


def out_cells():
    cells = [(a, x, y) for a in range(3) for x in range(4) for y in range(8)]
    cells += [(a, 4, y) for a in range(3) for y in range(8)]
    cells += [(a, x, 8) for x in range(4) for a in range(3)]
    cells += [(a, 4, 8) for a in range(3)]
    cells += [(a, 4, -1) for a in range(3)]
    return cells


def stencil_matrix():
    whole = np.zeros((3, ROWS, 96), np.float64)
    for part, step_z in enumerate((0, 1, -1)):
        for row, (a, x, y) in enumerate(out_cells()):
            for p in (-1, 0, 1):
                for r in (-1, 0, 1):
                    o = (p, r, step_z)
                    q = sum(v * v for v in o)
                    if q == 0 or not (0 <= x + p < 4 and 0 <= y + r < 8):
                        continue
                    for b in range(3):
                        g = (1.0 if a == b else 0.0) + 0.5 / q * o[a] * o[b]
                        whole[part, row, b * 32 + (x + p) * 8 + y + r] += 24.0 * 0.5 ** (q - 1) * g
    whole = np.round(whole).reshape(3 * ROWS, 96)
    return np.concatenate([whole, whole], axis=1)


def split(value):
    high = value.astype(BF16)
    low = (value - high.astype(F32)).astype(BF16)
    return jnp.concatenate([high, low], axis=0)


def dot(a, b):
    return lax.dot_general(a, b, (((1,), (0,)), ((), ())), preferred_element_type=F32)


def dot_nt(a, b):
    return lax.dot_general(a, b, (((1,), (1,)), ((), ())), preferred_element_type=F32)


def quadrants(r):
    top = r[:32] + r[32:]
    return top[:, :32] + top[:, 32:]


def kernel(basis, material, table, stencil, factor, panel,
           zs, mat, c_all, fb, rb, ks, packy, gin, gout, khx, khy, khc, ke, kd, kt, k3,
           ss, sgk, qb, nin, fin, bout, bin_,
           lsem, gs, gr, hs, hr, fs, fr, ns, nr, es, er, bs, br):
    s = lax.axis_index("sub")
    g = lax.axis_index("grp")
    i = s // YDOMS
    j = lax.rem(s, YDOMS)

    def near(p, r):
        return lax.rem(i + p + XDOMS, XDOMS) * YDOMS + lax.rem(j + r + YDOMS, YDOMS)

    def inside(p, r):
        ok = jnp.bool_(True)
        if p:
            ok = jnp.logical_and(ok, i < XDOMS - 1 if p > 0 else i > 0)
        if r:
            ok = jnp.logical_and(ok, j < YDOMS - 1 if r > 0 else j > 0)
        return ok

    def slab(d):
        return lax.rem(g + d + SLABS, SLABS)

    def remote(src, dst, send, recv, sub, grp):
        return pltpu.make_async_remote_copy(
            src_ref=src, dst_ref=dst, send_sem=send, recv_sem=recv,
            device_id={"sub": sub, "grp": grp}, device_id_type=MESH)

    load_mat = pltpu.make_async_copy(material, mat, lsem.at[0])
    load_zs = pltpu.make_async_copy(basis, zs, lsem.at[1])
    load_c = pltpu.make_async_copy(stencil, c_all, lsem.at[2])
    load_mat.start()
    load_zs.start()
    load_c.start()
    barrier = pltpu.get_barrier_semaphore()
    for p, r in ALL_NEAR:
        pl.semaphore_signal(barrier, inc=1, device_id={"sub": near(p, r), "grp": g}, device_id_type=MESH)
    for d in (1, 2, 3):
        pl.semaphore_signal(barrier, inc=1, device_id={"sub": s, "grp": slab(d)}, device_id_type=MESH)

    load_mat.wait()
    ids = mat[...]
    kappa = jnp.zeros((32, 128), F32)
    for which in range(8):
        kappa = kappa + jnp.where(ids == which, table[which], 0.0)
    ks[0] = kappa
    for a in range(3):
        k3[32 * a : 32 * a + 32, :] = kappa
    gout[0, 0:32, :] = kappa
    gout[1, 0:32, :] = kappa

    load_zs.wait()
    for a in range(3):
        for y in range(8):
            fb[8 * a + y] = zs[pl.ds(a * 1024 + y, 32, stride=32), :]
    for x in range(4):
        for a in range(3):
            fb[24 + 3 * x + a] = zs[pl.ds(a * 1024 + x * 8, 32, stride=32), :]
    for a in range(3):
        fb[36 + a] = zs[pl.ds(a * 1024 + 7, 32, stride=32), :]

    lane24 = lax.broadcasted_iota(jnp.int32, (24, 128), 1)

    def own(col):
        return jnp.concatenate(
            [zs[pl.ds(pl.multiple_of(a * 1024 + col * 32, 32), 32), :] for a in range(3)], axis=0)

    def edge(col, carry):
        first, last = carry
        u = own(col)
        for k in range(4):
            rows = u[24 * k : 24 * k + 24]
            here = lane24 == 32 * k + col
            first = jnp.where(here, pltpu.roll(rows, 32 * k + col, 1), first)
            last = jnp.where(here, pltpu.roll(rows, lax.rem(32 * k + col + 1, 128), 1), last)
        return first, last

    zero24 = jnp.zeros((24, 128), F32)
    first, last = lax.fori_loop(0, 32, edge, (zero24, zero24))
    gout[0, 32:56, :] = first
    gout[1, 32:56, :] = last

    pl.semaphore_wait(barrier, len(ALL_NEAR) + 3)

    to_low = remote(gout.at[0], gin.at[1], gs.at[0], gr.at[1], s, slab(-1))
    to_high = remote(gout.at[1], gin.at[0], gs.at[1], gr.at[0], s, slab(1))
    to_low.start()
    to_high.start()
    faces = []
    for a in range(3):
        faces.append(remote(fb.at[pl.ds(8 * a, 8)], rb.at[pl.ds(8 * a, 8)], fs.at[a], fr.at[a], near(-1, 0), g))
    faces.append(remote(fb.at[pl.ds(24, 12)], rb.at[pl.ds(24, 12)], fs.at[3], fr.at[3], near(0, -1), g))
    faces.append(remote(fb.at[pl.ds(24, 3)], rb.at[pl.ds(36, 3)], fs.at[4], fr.at[4], near(-1, -1), g))
    faces.append(remote(fb.at[pl.ds(36, 3)], rb.at[pl.ds(39, 3)], fs.at[5], fr.at[5], near(-1, 1), g))
    for copy in faces:
        copy.start()

    to_low.wait_recv()
    to_high.wait_recv()
    lane = lax.broadcasted_iota(jnp.int32, (32, 128), 1)
    low_ok = g > 0
    high_ok = g < SLABS - 1
    k_low = jnp.where(low_ok, gin[0, 0:32, :], 0.0)
    k_high = jnp.where(high_ok, gin[1, 0:32, :], 0.0)
    k_down = jnp.where(lane == 0, pltpu.roll(k_low, 1, 1), pltpu.roll(kappa, 1, 1))
    k_up = jnp.where(lane == 127, pltpu.roll(k_high, 127, 1), pltpu.roll(kappa, 127, 1))
    ks[1] = kappa + 0.5 * (k_down + k_up)
    for e, y in ((0, 0), (1, 7)):
        for which in range(2):
            for x in range(4):
                packy[e, 4 * which + x : 4 * which + x + 1, :] = ks[which, 8 * x + y : 8 * x + y + 1, :]
    halo = [
        remote(ks.at[:, pl.ds(0, 8)], khx.at[1], hs.at[0], hr.at[0], near(-1, 0), g),
        remote(ks.at[:, pl.ds(24, 8)], khx.at[0], hs.at[1], hr.at[1], near(1, 0), g),
        remote(packy.at[0], khy.at[1], hs.at[2], hr.at[2], near(0, -1), g),
        remote(packy.at[1], khy.at[0], hs.at[3], hr.at[3], near(0, 1), g),
        remote(packy.at[0], khc.at[3], hs.at[4], hr.at[4], near(-1, -1), g),
        remote(packy.at[1], khc.at[0], hs.at[5], hr.at[5], near(1, 1), g),
        remote(packy.at[1], khc.at[2], hs.at[6], hr.at[6], near(-1, 1), g),
        remote(packy.at[0], khc.at[1], hs.at[7], hr.at[7], near(1, -1), g),
    ]
    for copy in halo:
        copy.start()

    load_c.wait()
    lane96 = lax.broadcasted_iota(jnp.int32, (96, 128), 1)

    def spread(packed):
        return jnp.concatenate(
            [packed if k == 0 else pltpu.roll(packed, 128 - 32 * k, 1) for k in range(4)], axis=0)

    h_high = spread(jnp.where(high_ok, gin[1, 32:56, :], 0.0))
    h_low = spread(jnp.where(low_ok, gin[0, 32:56, :], 0.0))
    kc_high = jnp.concatenate([k_high[:, 0:1]] * 3, axis=0)
    kc_low = jnp.concatenate([k_low[:, 127:128]] * 3, axis=0)
    edges = jnp.where(lane96 < 32, h_high, pltpu.roll(h_low, 32, 1))
    kedges = jnp.where(lane96 < 32, h_high * kc_high, pltpu.roll(h_low * kc_low, 32, 1))
    edges = jnp.where(lane96 < 64, edges, pltpu.roll(kedges, 64, 1))
    ch = dot(c_all[...], split(edges))
    ch_high = ch[ROWS : 2 * ROWS]
    ch_low = ch[2 * ROWS : 3 * ROWS]
    lane_all = lax.broadcasted_iota(jnp.int32, (ROWS, 128), 1)
    lane48 = lax.broadcasted_iota(jnp.int32, (48, 128), 1)
    kpair = jnp.concatenate([k3[...], k3[...]], axis=1)
    c_ghost = jnp.concatenate([c_all[part * ROWS + 96 : (part + 1) * ROWS, :] for part in range(3)], axis=0)

    def pair(step, carry):
        u = jnp.concatenate([own(2 * step), own(2 * step + 1)], axis=1)
        r = dot(c_all[...], split(u))
        rk = dot(c_ghost, split(u * kpair))
        for half in range(2):
            col = 2 * step + half
            part = r[:, 128 * half : 128 * half + 128]
            up = jnp.where(lane_all == 127, pltpu.roll(ch_high, 127 - col, 1), pltpu.roll(part[ROWS : 2 * ROWS], 127, 1))
            down = jnp.where(lane_all == 0, pltpu.roll(ch_low, 96 - col, 1), pltpu.roll(part[2 * ROWS :], 1, 1))
            ss[pl.ds(pl.multiple_of(col * ROWS, ROWS), ROWS), :] = part[:ROWS] + up + down
            part = rk[:, 128 * half : 128 * half + 128]
            up = jnp.where(lane48 == 127, pltpu.roll(ch_high[96:], 63 - col, 1), pltpu.roll(part[48:96], 127, 1))
            down = jnp.where(lane48 == 0, pltpu.roll(ch_low[96:], 32 - col, 1), pltpu.roll(part[96:], 1, 1))
            sgk[pl.ds(pl.multiple_of(col * 48, 48), 48), :] = part[:48] + up + down
        return carry

    lax.fori_loop(0, 16, pair, 0)

    for copy in halo:
        copy.wait_recv()
    ke[...] = jnp.zeros_like(ke)
    for x in range(4):
        ke[1 + x, 1:9, :] = ks[1, 8 * x : 8 * x + 8, :]
        ke[1 + x, 0:1, :] = jnp.where(inside(0, -1), khy[0, 4 + x : 5 + x, :], 0.0)
        ke[1 + x, 9:10, :] = jnp.where(inside(0, 1), khy[1, 4 + x : 5 + x, :], 0.0)
    ke[0, 1:9, :] = jnp.where(inside(-1, 0), khx[0, 1], 0.0)
    ke[5, 1:9, :] = jnp.where(inside(1, 0), khx[1, 1], 0.0)
    ke[0, 0:1, :] = jnp.where(inside(-1, -1), khc[0, 7:8, :], 0.0)
    ke[0, 9:10, :] = jnp.where(inside(-1, 1), khc[1, 7:8, :], 0.0)
    ke[5, 0:1, :] = jnp.where(inside(1, -1), khc[2, 4:5, :], 0.0)
    ke[5, 9:10, :] = jnp.where(inside(1, 1), khc[3, 4:5, :], 0.0)
    planes = [ke[x, 1:9, :] + 0.5 * (ke[x, 0:8, :] + ke[x, 2:10, :]) for x in range(6)]
    for x in range(4):
        smooth = planes[x + 1] + 0.5 * (planes[x] + planes[x + 2])
        kd[8 * x : 8 * x + 8, :] = 228.0 * ks[0, 8 * x : 8 * x + 8, :] + 36.0 * smooth
    for a in range(3):
        kt[8 * a : 8 * a + 8, :] = khx[1, 0]
        for x in range(4):
            kt[24 + 3 * x + a : 25 + 3 * x + a, :] = khy[1, x : x + 1, :]
        kt[36 + a : 37 + a, :] = khc[3, 0:1, :]
        kt[39 + a : 40 + a, :] = khc[2, 0:1, :]
    kt[42:48, :] = jnp.zeros((6, 128), F32)

    def inner(step, total):
        start_z = (step // 4) * 1024 + lax.rem(step, 4) * 8
        start_s = step * 8
        start_k = lax.rem(step, 4) * 8
        left, right = [], []
        for y in range(8):
            z = zs[pl.ds(start_z + y, 32, stride=32), :]
            v = ss[pl.ds(start_s + y, 32, stride=ROWS), :]
            left.append(z)
            right.append(kd[pl.ds(start_k + y, 1), :] * z - ks[0, pl.ds(start_k + y, 1), :] * v)
        left = split(jnp.concatenate(left, axis=1))
        right = split(jnp.concatenate(right, axis=1))
        return total + dot_nt(left, right)

    total = quadrants(lax.fori_loop(0, 12, inner, jnp.zeros((64, 64), F32)))
    total = (total + total.T) * (1.0 / 48.0)
    nin[g, :, 0:32] = total
    sums = [remote(nin.at[g], nin.at[g], ns.at[d - 1], nr.at[d - 1], s, slab(d)) for d in (1, 2, 3)]
    for copy in sums:
        copy.start()

    def ghost(step, carry):
        tiles = []
        for y in range(8):
            m = step * 8 + y
            tiles.append(kt[pl.ds(m, 1), :] * ss[pl.ds(96 + m, 32, stride=ROWS), :] + sgk[pl.ds(m, 32, stride=48), :])
        qb[:, pl.ds(pl.multiple_of(step * 1024, 1024), 1024)] = split(jnp.concatenate(tiles, axis=1))
        return carry

    lax.fori_loop(0, 6, ghost, 0)

    def coupled(start, count):
        f = split(jnp.concatenate([rb[start + t] for t in range(count)], axis=1))
        return dot_nt(qb[:, start * 128 : (start + count) * 128], f)

    lane32 = lax.broadcasted_iota(jnp.int32, (32, 128), 1)
    lane8 = lax.broadcasted_iota(jnp.int32, (8, 128), 1)

    def place(parts):
        result = jnp.zeros((32, 128), F32)
        for at, block in parts.items():
            wide = jnp.concatenate([block, jnp.zeros((32, 96), F32)], axis=1)
            wide = wide if at == 0 else pltpu.roll(wide, 32 * at, 1)
            result = jnp.where(lane32 // 32 == at, wide, result)
        return result

    def turned(block):
        wide = jnp.concatenate([block.T, jnp.zeros((32, 96), F32)], axis=1)
        result = wide[0:8]
        for k in range(1, 4):
            result = jnp.where(lane8 // 32 == k, pltpu.roll(wide[8 * k : 8 * k + 8], 32 * k, 1), result)
        return result

    sent = []

    def give(which, at, blocks):
        tile = place(blocks)
        fin[which, g] = tile
        for d in (1, 2, 3):
            copy = remote(fin.at[which, g], fin.at[which, g], es.at[which, d - 1], er.at[which, d - 1], s, slab(d))
            copy.start()
            sent.append(copy)
        for b, block in blocks.items():
            bout[b] = turned(block)
            for d in range(4):
                copy = remote(bout.at[b], bin_.at[b, g], bs.at[b, d], br.at[b, d], near(*FORWARD[b]), slab(d))
                copy.start()
                sent.append(copy)

    def finished(b, value):
        return jnp.where(inside(*FORWARD[b]), quadrants(value) * (-1.0 / 48.0), 0.0)

    for which in (3, 4, 5):
        faces[which].wait_recv()
    give(0, 0, {0: finished(0, coupled(24, 12)), 1: finished(1, coupled(39, 3)), 3: finished(3, coupled(36, 3))})
    value = jnp.zeros((64, 64), F32)
    for a in range(3):
        faces[a].wait_recv()
        value = value + coupled(8 * a, 8)
    give(1, 2, {2: finished(2, value)})

    for copy in sums:
        copy.wait_recv()
    row32 = lax.broadcasted_iota(jnp.int32, (32, 128), 0)
    m = nin[0] + nin[1] + nin[2] + nin[3]
    m = jnp.where(lane32 < 32, m, jnp.where(lane32 == row32 + 32, 1.0, 0.0))
    lower = jnp.zeros((32, 128), F32)
    for k in range(32):
        pivot = m[k : k + 1, k : k + 1]
        r = lax.rsqrt(pivot)
        r = r * (1.5 - 0.5 * pivot * r * r)
        col = m[:, k : k + 1] * r
        line = m[k : k + 1, :] * r
        lower = jnp.where(jnp.logical_and(lane32 == k, row32 >= k), col, lower)
        m = jnp.where(row32 > k, m - col * line, jnp.where(row32 == k, line, m))
    factor[...] = lower[:, 0:32] * (1.0 / np.sqrt(49152.0))
    inverse = m[:, 32:64]

    for copy in sent:
        copy.wait_recv()
    ahead = jnp.zeros((32, 128), F32)
    for h in range(SLABS):
        ahead = ahead + (fin[0, h] + fin[1, h])
    behind = [jnp.zeros((8, 128), F32)] * 4
    packed = [bin_[b, 0] + bin_[b, 1] + bin_[b, 2] + bin_[b, 3] for b in range(4)]
    order = [3, 2, 1, 0]
    rows = []
    for k in range(4):
        result = jnp.zeros((8, 128), F32)
        for at in range(4):
            shift = (32 * (at - k)) % 128
            moved = packed[order[at]] if shift == 0 else pltpu.roll(packed[order[at]], shift, 1)
            result = jnp.where(lane8 // 32 == at, moved, result)
        rows.append(result)
    every = jnp.concatenate([jnp.concatenate(rows, axis=0), ahead], axis=1)
    panel[...] = lax.dot_general(inverse, every, (((1,), (0,)), ((), ())), precision=lax.Precision.HIGHEST,
                                 preferred_element_type=F32)

    to_low.wait_send()
    to_high.wait_send()
    for copy in faces + halo + sums + sent:
        copy.wait_send()


def shards(stencil, basis, material, kappa_table):
    any_space = pl.BlockSpec(memory_space=pl.ANY)
    vmem = pl.BlockSpec(memory_space=pltpu.VMEM)
    dma = pltpu.SemaphoreType.DMA
    factor, panel = pl.pallas_call(
        kernel,
        out_shape=(jax.ShapeDtypeStruct((32, 32), F32), jax.ShapeDtypeStruct((32, 256), F32)),
        in_specs=[any_space, any_space, pl.BlockSpec(memory_space=pltpu.SMEM), any_space],
        out_specs=(vmem, vmem),
        scratch_shapes=[
            pltpu.VMEM((3072, 128), F32),
            pltpu.VMEM((32, 128), jnp.int32),
            pltpu.VMEM((3 * ROWS, 192), BF16),
            pltpu.VMEM((39, 32, 128), F32),
            pltpu.VMEM((42, 32, 128), F32),
            pltpu.VMEM((2, 32, 128), F32),
            pltpu.VMEM((2, 8, 128), F32),
            pltpu.VMEM((2, 56, 128), F32),
            pltpu.VMEM((2, 56, 128), F32),
            pltpu.VMEM((2, 2, 8, 128), F32),
            pltpu.VMEM((2, 8, 128), F32),
            pltpu.VMEM((4, 8, 128), F32),
            pltpu.VMEM((6, 16, 128), F32),
            pltpu.VMEM((32, 128), F32),
            pltpu.VMEM((48, 128), F32),
            pltpu.VMEM((96, 128), F32),
            pltpu.VMEM((32 * ROWS, 128), F32),
            pltpu.VMEM((32 * 48, 128), F32),
            pltpu.VMEM((64, 6 * 1024), BF16),
            pltpu.VMEM((4, 32, 128), F32),
            pltpu.VMEM((2, 4, 32, 128), F32),
            pltpu.VMEM((4, 8, 128), F32),
            pltpu.VMEM((4, 4, 8, 128), F32),
            dma((3,)), dma((2,)), dma((2,)), dma((8,)), dma((8,)), dma((6,)), dma((6,)),
            dma((3,)), dma((3,)), dma((2, 3)), dma((2, 3)), dma((4, 4)), dma((4, 4)),
        ],
        compiler_params=pltpu.CompilerParams(
            collective_id=0, has_side_effects=True, vmem_limit_bytes=40 * 2**20),
        name="coarse_blocks",
    )(basis.reshape(3072, 128), material.reshape(32, 128), kappa_table, stencil)
    panel = panel.reshape(32, 8, 32).transpose(1, 0, 2)
    return factor[None], panel[None]


def solution(mesh):
    placed = (P(), P("sub", None, None, None, None, "grp"), P("sub", None, None, "grp"), P())
    call = jax.shard_map(
        shards,
        mesh=mesh,
        in_specs=placed,
        out_specs=(P("sub", None, None), P("sub", None, None, None)),
        check_vma=False,
    )
    matrix = stencil_matrix()

    def run(basis, material, kappa_table):
        return call(jnp.asarray(matrix, BF16), basis, material, kappa_table)

    return run
```

time: 206 us -> 48.7 us (0.24)
  the two profiles are of different devices: /device:TPU:6 before, /device:TPU:1 now
where the time goes in v1:
time: 48.7 us; the launch traced here: 48.5 us
  Pallas kernels  42.7 us (88%)
  local copies, waits for them, and re-layouts  5.08 us (10%)
  between operations  0.66 us (1%)
    pallas_call x1, Pallas kernels, shards(): pl.pallas_call(kernel, out_shape=(jax.ShapeDtypeStruct((32, 32), F32), ja...  42.7 us
    unnamed x9, local copies, waits for them, and re-layouts  4.31 us

profile of v1, /device:TPU:1, one launch (start us, length us, event | category | flops | bytes accessed | tf_op | source)
XLA Modules:
  0.0 48.5 jit_solution(7390656658547200232)
XLA Ops:
  0.6 0.0 copy-start
  0.6 1.4 %copy-done = f32[1,3,32,4,8,128]{5,4,3,2,1,0:T(8,128)S(1)} copy-done((f32[1,3,32,4,8,128]{5,4,3,2,1,0:T(8,128)S(1)}, f32[1,3,32,4,8,128]{5,4,3,2,1,0:T(8,128)}, u32[]{:S(2)}) %copy-start) | copy-done | bytes 1572888
  2.0 0.0 copy-start.1
  2.0 0.9 %copy-done.1 = bf16[432,192]{1,0:T(8,128)(2,1)S(1)} copy-done((bf16[432,192]{1,0:T(8,128)(2,1)S(1)}, bf16[432,192]{1,0:T(8,128)(2,1)}, u32[]{:S(2)}) %copy-start.1) | copy-done | bytes 165912
  3.0 0.0 copy-start.2
  3.0 0.7 %copy-done.2 = s32[1,4,8,128]{3,2,1,0:T(8,128)S(1)} copy-done((s32[1,4,8,128]{3,2,1,0:T(8,128)S(1)}, s32[1,4,8,128]{3,2,1,0:T(8,128)}, u32[]{:S(2)}) %copy-start.2) | copy-done | bytes 16408
  3.7 0.0 copy-start.3
  3.7 0.7 %copy-done.3 = f32[8]{0:T(128)S(1)} copy-done((f32[8]{0:T(128)S(1)}, f32[8]{0:T(128)}, u32[]{:S(2)}) %copy-start.3) | copy-done | bytes 56
  4.3 42.7 %coarse_blocks.1 = (f32[32,32]{1,0:T(8,128)S(1)}, f32[32,256]{1,0:T(8,128)S(1)}) custom-call(f32[3072,128]{1,0:T(8,128)S(1)} %bitcast.8, s32[32,128]{1,0:T(8,128)S(1)} %bitcast.9, f32[8]{0:T(128)S(1)} %copy-done.3, bf16[432,192]{1,0:T(8,128)(2,1)S(1)} %copy-done.1), custom_call_target="tpu_custom_call" | custom-call | tf_op jit(solution)/shard_map/coarse_blocks/pallas_call | solution.py:385
  47.1 0.1 reshape.15
  47.2 0.7 %copy.8 = f32[32,8,32]{2,0,1:T(8,128)} copy(f32[32,8,32]{2,1,0:T(8,128)S(1)} %reshape.15) | data formatting | bytes 65536 | tf_op jit(solution)/shard_map/reshape | solution.py:421
  47.9 0.6 %copy.10 = f32[1,32,32]{2,1,0:T(8,128)} copy(f32[1,32,32]{2,1,0:T(8,128)S(1)} %bitcast.10) | data formatting | bytes 8192
Async XLA Ops:
  0.6 1.4 %copy-start = (f32[1,3,32,4,8,128]{5,4,3,2,1,0:T(8,128)S(1)}, f32[1,3,32,4,8,128]{5,4,3,2,1,0:T(8,128)}, u32[]{:S(2)}) copy-start(f32[1,3,32,4,8,128]{5,4,3,2,1,0:T(8,128)} %param.4) | copy-start | bytes 4718596
  2.0 0.9 %copy-start.1 = (bf16[432,192]{1,0:T(8,128)(2,1)S(1)}, bf16[432,192]{1,0:T(8,128)(2,1)}, u32[]{:S(2)}) copy-start(bf16[432,192]{1,0:T(8,128)(2,1)} %constant.2.clone.stencil) | copy-start | bytes 497668
  3.0 0.7 %copy-start.2 = (s32[1,4,8,128]{3,2,1,0:T(8,128)S(1)}, s32[1,4,8,128]{3,2,1,0:T(8,128)}, u32[]{:S(2)}) copy-start(s32[1,4,8,128]{3,2,1,0:T(8,128)} %param.5) | copy-start | bytes 49156
  3.7 0.7 %copy-start.3 = (f32[8]{0:T(128)S(1)}, f32[8]{0:T(128)}, u32[]{:S(2)}) copy-start(f32[8]{0:T(128)} %table.1) | copy-start | bytes 100

commit v2 on v1

--- a/solution.py
+++ b/solution.py
@@ -60,6 +60,10 @@
     return lax.dot_general(a, b, (((1,), (1,)), ((), ())), preferred_element_type=F32)
 
 
+def dot_tn(a, b):
+    return lax.dot_general(a, b, (((0,), (0,)), ((), ())), precision=lax.Precision.HIGHEST, preferred_element_type=F32)
+
+
 def quadrants(r):
     top = r[:32] + r[32:]
     return top[:, :32] + top[:, 32:]
@@ -67,7 +71,7 @@
 
 def kernel(basis, material, table, stencil, factor, panel,
            zs, mat, c_all, fb, rb, ks, packy, gin, gout, khx, khy, khc, ke, kd, kt, k3,
-           ss, sgk, qb, nin, fin, bout, bin_,
+           ss, sgk, qb, nin, fin, bout, bin_, tab, c_in,
            lsem, gs, gr, hs, hr, fs, fr, ns, nr, es, er, bs, br):
     s = lax.axis_index("sub")
     g = lax.axis_index("grp")
@@ -93,24 +97,31 @@
             src_ref=src, dst_ref=dst, send_sem=send, recv_sem=recv,
             device_id={"sub": sub, "grp": grp}, device_id_type=MESH)
 
-    load_mat = pltpu.make_async_copy(material, mat, lsem.at[0])
-    load_zs = pltpu.make_async_copy(basis, zs, lsem.at[1])
-    load_c = pltpu.make_async_copy(stencil, c_all, lsem.at[2])
-    load_mat.start()
-    load_zs.start()
-    load_c.start()
     barrier = pltpu.get_barrier_semaphore()
     for p, r in ALL_NEAR:
         pl.semaphore_signal(barrier, inc=1, device_id={"sub": near(p, r), "grp": g}, device_id_type=MESH)
     for d in (1, 2, 3):
         pl.semaphore_signal(barrier, inc=1, device_id={"sub": s, "grp": slab(d)}, device_id_type=MESH)
 
+    load_mat = pltpu.make_async_copy(material, mat, lsem.at[0])
+    load_zs = pltpu.make_async_copy(basis, zs, lsem.at[1])
+    load_c = pltpu.make_async_copy(stencil, c_in, lsem.at[2])
+    load_tab = pltpu.make_async_copy(table, tab, lsem.at[3])
+    load_mat.start()
+    load_tab.start()
+    load_zs.start()
+    load_c.start()
+
     load_mat.wait()
+    load_tab.wait()
     ids = mat[...]
     kappa = jnp.zeros((32, 128), F32)
     for which in range(8):
-        kappa = kappa + jnp.where(ids == which, table[which], 0.0)
-    ks[0] = kappa
+        kappa = kappa + jnp.where(ids == which, tab[which], 0.0)
+    ks[...] = kappa
+    for e, y in ((0, 0), (1, 7)):
+        for x in range(4):
+            packy[e, x : x + 1, :] = ks[8 * x + y : 8 * x + y + 1, :]
     for a in range(3):
         k3[32 * a : 32 * a + 32, :] = kappa
     gout[0, 0:32, :] = kappa
@@ -147,38 +158,17 @@
     gout[0, 32:56, :] = first
     gout[1, 32:56, :] = last
 
+    load_c.wait()
+    c_all[...] = c_in[...].astype(BF16)
     pl.semaphore_wait(barrier, len(ALL_NEAR) + 3)
 
     to_low = remote(gout.at[0], gin.at[1], gs.at[0], gr.at[1], s, slab(-1))
     to_high = remote(gout.at[1], gin.at[0], gs.at[1], gr.at[0], s, slab(1))
     to_low.start()
     to_high.start()
-    faces = []
-    for a in range(3):
-        faces.append(remote(fb.at[pl.ds(8 * a, 8)], rb.at[pl.ds(8 * a, 8)], fs.at[a], fr.at[a], near(-1, 0), g))
-    faces.append(remote(fb.at[pl.ds(24, 12)], rb.at[pl.ds(24, 12)], fs.at[3], fr.at[3], near(0, -1), g))
-    faces.append(remote(fb.at[pl.ds(24, 3)], rb.at[pl.ds(36, 3)], fs.at[4], fr.at[4], near(-1, -1), g))
-    faces.append(remote(fb.at[pl.ds(36, 3)], rb.at[pl.ds(39, 3)], fs.at[5], fr.at[5], near(-1, 1), g))
-    for copy in faces:
-        copy.start()
-
-    to_low.wait_recv()
-    to_high.wait_recv()
-    lane = lax.broadcasted_iota(jnp.int32, (32, 128), 1)
-    low_ok = g > 0
-    high_ok = g < SLABS - 1
-    k_low = jnp.where(low_ok, gin[0, 0:32, :], 0.0)
-    k_high = jnp.where(high_ok, gin[1, 0:32, :], 0.0)
-    k_down = jnp.where(lane == 0, pltpu.roll(k_low, 1, 1), pltpu.roll(kappa, 1, 1))
-    k_up = jnp.where(lane == 127, pltpu.roll(k_high, 127, 1), pltpu.roll(kappa, 127, 1))
-    ks[1] = kappa + 0.5 * (k_down + k_up)
-    for e, y in ((0, 0), (1, 7)):
-        for which in range(2):
-            for x in range(4):
-                packy[e, 4 * which + x : 4 * which + x + 1, :] = ks[which, 8 * x + y : 8 * x + y + 1, :]
     halo = [
-        remote(ks.at[:, pl.ds(0, 8)], khx.at[1], hs.at[0], hr.at[0], near(-1, 0), g),
-        remote(ks.at[:, pl.ds(24, 8)], khx.at[0], hs.at[1], hr.at[1], near(1, 0), g),
+        remote(ks.at[pl.ds(0, 8)], khx.at[1], hs.at[0], hr.at[0], near(-1, 0), g),
+        remote(ks.at[pl.ds(24, 8)], khx.at[0], hs.at[1], hr.at[1], near(1, 0), g),
         remote(packy.at[0], khy.at[1], hs.at[2], hr.at[2], near(0, -1), g),
         remote(packy.at[1], khy.at[0], hs.at[3], hr.at[3], near(0, 1), g),
         remote(packy.at[0], khc.at[3], hs.at[4], hr.at[4], near(-1, -1), g),
@@ -188,8 +178,22 @@
     ]
     for copy in halo:
         copy.start()
-
-    load_c.wait()
+    faces = []
+    for a in range(3):
+        faces.append(remote(fb.at[pl.ds(8 * a, 8)], rb.at[pl.ds(8 * a, 8)], fs.at[a], fr.at[a], near(-1, 0), g))
+    faces.append(remote(fb.at[pl.ds(24, 12)], rb.at[pl.ds(24, 12)], fs.at[3], fr.at[3], near(0, -1), g))
+    faces.append(remote(fb.at[pl.ds(24, 3)], rb.at[pl.ds(36, 3)], fs.at[4], fr.at[4], near(-1, -1), g))
+    faces.append(remote(fb.at[pl.ds(36, 3)], rb.at[pl.ds(39, 3)], fs.at[5], fr.at[5], near(-1, 1), g))
+    for copy in faces:
+        copy.start()
+
+    to_low.wait_recv()
+    to_high.wait_recv()
+    lane = lax.broadcasted_iota(jnp.int32, (32, 128), 1)
+    low_ok = g > 0
+    high_ok = g < SLABS - 1
+    k_low = jnp.where(low_ok, gin[0, 0:32, :], 0.0)
+    k_high = jnp.where(high_ok, gin[1, 0:32, :], 0.0)
     lane96 = lax.broadcasted_iota(jnp.int32, (96, 128), 1)
 
     def spread(packed):
@@ -233,26 +237,43 @@
         copy.wait_recv()
     ke[...] = jnp.zeros_like(ke)
     for x in range(4):
-        ke[1 + x, 1:9, :] = ks[1, 8 * x : 8 * x + 8, :]
-        ke[1 + x, 0:1, :] = jnp.where(inside(0, -1), khy[0, 4 + x : 5 + x, :], 0.0)
-        ke[1 + x, 9:10, :] = jnp.where(inside(0, 1), khy[1, 4 + x : 5 + x, :], 0.0)
-    ke[0, 1:9, :] = jnp.where(inside(-1, 0), khx[0, 1], 0.0)
-    ke[5, 1:9, :] = jnp.where(inside(1, 0), khx[1, 1], 0.0)
-    ke[0, 0:1, :] = jnp.where(inside(-1, -1), khc[0, 7:8, :], 0.0)
-    ke[0, 9:10, :] = jnp.where(inside(-1, 1), khc[1, 7:8, :], 0.0)
-    ke[5, 0:1, :] = jnp.where(inside(1, -1), khc[2, 4:5, :], 0.0)
-    ke[5, 9:10, :] = jnp.where(inside(1, 1), khc[3, 4:5, :], 0.0)
+        ke[1 + x, 1:9, :] = ks[8 * x : 8 * x + 8, :]
+        ke[1 + x, 0:1, :] = jnp.where(inside(0, -1), khy[0, x : 1 + x, :], 0.0)
+        ke[1 + x, 9:10, :] = jnp.where(inside(0, 1), khy[1, x : 1 + x, :], 0.0)
+    ke[0, 1:9, :] = jnp.where(inside(-1, 0), khx[0], 0.0)
+    ke[5, 1:9, :] = jnp.where(inside(1, 0), khx[1], 0.0)
+    ke[0, 0:1, :] = jnp.where(inside(-1, -1), khc[0, 3:4, :], 0.0)
+    ke[0, 9:10, :] = jnp.where(inside(-1, 1), khc[1, 3:4, :], 0.0)
+    ke[5, 0:1, :] = jnp.where(inside(1, -1), khc[2, 0:1, :], 0.0)
+    ke[5, 9:10, :] = jnp.where(inside(1, 1), khc[3, 0:1, :], 0.0)
     planes = [ke[x, 1:9, :] + 0.5 * (ke[x, 0:8, :] + ke[x, 2:10, :]) for x in range(6)]
-    for x in range(4):
-        smooth = planes[x + 1] + 0.5 * (planes[x] + planes[x + 2])
-        kd[8 * x : 8 * x + 8, :] = 228.0 * ks[0, 8 * x : 8 * x + 8, :] + 36.0 * smooth
-    for a in range(3):
-        kt[8 * a : 8 * a + 8, :] = khx[1, 0]
+    smooth = jnp.concatenate([planes[x + 1] + 0.5 * (planes[x] + planes[x + 2]) for x in range(4)], axis=0)
+    up = jnp.where(lane == 127, 0.0, pltpu.roll(smooth, 127, 1))
+    down = jnp.where(lane == 0, 0.0, pltpu.roll(smooth, 1, 1))
+    kd[...] = 228.0 * ks[...] + 36.0 * smooth + 18.0 * (up + down)
+    for a in range(3):
+        kt[8 * a : 8 * a + 8, :] = khx[1]
         for x in range(4):
             kt[24 + 3 * x + a : 25 + 3 * x + a, :] = khy[1, x : x + 1, :]
         kt[36 + a : 37 + a, :] = khc[3, 0:1, :]
         kt[39 + a : 40 + a, :] = khc[2, 0:1, :]
     kt[42:48, :] = jnp.zeros((6, 128), F32)
+
+    near_low = jnp.concatenate([smooth[:, 0:1]] * 3, axis=0) * 18.0
+    near_high = jnp.concatenate([smooth[:, 127:128]] * 3, axis=0) * 18.0
+    layers = jnp.concatenate([h_low, h_high], axis=0)
+    weighted = jnp.concatenate([h_low * near_low, h_high * near_high], axis=0)
+    outside = dot_tn(weighted, layers)[:32, :32]
+
+    def ghost(step, carry):
+        tiles = []
+        for y in range(8):
+            m = step * 8 + y
+            tiles.append(kt[pl.ds(m, 1), :] * ss[pl.ds(96 + m, 32, stride=ROWS), :] + sgk[pl.ds(m, 32, stride=48), :])
+        qb[:, pl.ds(pl.multiple_of(step * 1024, 1024), 1024)] = split(jnp.concatenate(tiles, axis=1))
+        return carry
+
+    lax.fori_loop(0, 6, ghost, 0)
 
     def inner(step, total):
         start_z = (step // 4) * 1024 + lax.rem(step, 4) * 8
@@ -263,27 +284,17 @@
             z = zs[pl.ds(start_z + y, 32, stride=32), :]
             v = ss[pl.ds(start_s + y, 32, stride=ROWS), :]
             left.append(z)
-            right.append(kd[pl.ds(start_k + y, 1), :] * z - ks[0, pl.ds(start_k + y, 1), :] * v)
+            right.append(kd[pl.ds(start_k + y, 1), :] * z - ks[pl.ds(start_k + y, 1), :] * v)
         left = split(jnp.concatenate(left, axis=1))
         right = split(jnp.concatenate(right, axis=1))
         return total + dot_nt(left, right)
 
-    total = quadrants(lax.fori_loop(0, 12, inner, jnp.zeros((64, 64), F32)))
+    total = quadrants(lax.fori_loop(0, 12, inner, jnp.zeros((64, 64), F32))) + outside
     total = (total + total.T) * (1.0 / 48.0)
     nin[g, :, 0:32] = total
     sums = [remote(nin.at[g], nin.at[g], ns.at[d - 1], nr.at[d - 1], s, slab(d)) for d in (1, 2, 3)]
     for copy in sums:
         copy.start()
-
-    def ghost(step, carry):
-        tiles = []
-        for y in range(8):
-            m = step * 8 + y
-            tiles.append(kt[pl.ds(m, 1), :] * ss[pl.ds(96 + m, 32, stride=ROWS), :] + sgk[pl.ds(m, 32, stride=48), :])
-        qb[:, pl.ds(pl.multiple_of(step * 1024, 1024), 1024)] = split(jnp.concatenate(tiles, axis=1))
-        return carry
-
-    lax.fori_loop(0, 6, ghost, 0)
 
     def coupled(start, count):
         f = split(jnp.concatenate([rb[start + t] for t in range(count)], axis=1))
@@ -379,13 +390,14 @@
 
 
 def shards(stencil, basis, material, kappa_table):
-    any_space = pl.BlockSpec(memory_space=pl.ANY)
+    hbm = pl.BlockSpec(memory_space=pltpu.HBM)
     vmem = pl.BlockSpec(memory_space=pltpu.VMEM)
     dma = pltpu.SemaphoreType.DMA
+    operands = (basis.reshape(3072, 128), material.reshape(32, 128), kappa_table, stencil)
     factor, panel = pl.pallas_call(
         kernel,
         out_shape=(jax.ShapeDtypeStruct((32, 32), F32), jax.ShapeDtypeStruct((32, 256), F32)),
-        in_specs=[any_space, any_space, pl.BlockSpec(memory_space=pltpu.SMEM), any_space],
+        in_specs=[hbm, hbm, hbm, hbm],
         out_specs=(vmem, vmem),
         scratch_shapes=[
             pltpu.VMEM((3072, 128), F32),
@@ -393,11 +405,11 @@
             pltpu.VMEM((3 * ROWS, 192), BF16),
             pltpu.VMEM((39, 32, 128), F32),
             pltpu.VMEM((42, 32, 128), F32),
-            pltpu.VMEM((2, 32, 128), F32),
+            pltpu.VMEM((32, 128), F32),
             pltpu.VMEM((2, 8, 128), F32),
             pltpu.VMEM((2, 56, 128), F32),
             pltpu.VMEM((2, 56, 128), F32),
-            pltpu.VMEM((2, 2, 8, 128), F32),
+            pltpu.VMEM((2, 8, 128), F32),
             pltpu.VMEM((2, 8, 128), F32),
             pltpu.VMEM((4, 8, 128), F32),
             pltpu.VMEM((6, 16, 128), F32),
@@ -411,13 +423,15 @@
             pltpu.VMEM((2, 4, 32, 128), F32),
             pltpu.VMEM((4, 8, 128), F32),
             pltpu.VMEM((4, 4, 8, 128), F32),
-            dma((3,)), dma((2,)), dma((2,)), dma((8,)), dma((8,)), dma((6,)), dma((6,)),
+            pltpu.SMEM((8,), F32),
+            pltpu.VMEM((3 * ROWS, 192), F32),
+            dma((4,)), dma((2,)), dma((2,)), dma((8,)), dma((8,)), dma((6,)), dma((6,)),
             dma((3,)), dma((3,)), dma((2, 3)), dma((2, 3)), dma((4, 4)), dma((4, 4)),
         ],
         compiler_params=pltpu.CompilerParams(
             collective_id=0, has_side_effects=True, vmem_limit_bytes=40 * 2**20),
         name="coarse_blocks",
-    )(basis.reshape(3072, 128), material.reshape(32, 128), kappa_table, stencil)
+    )(*(pltpu.with_memory_space_constraint(value, pltpu.HBM) for value in operands))
     panel = panel.reshape(32, 8, 32).transpose(1, 0, 2)
     return factor[None], panel[None]
 
@@ -434,6 +448,6 @@
     matrix = stencil_matrix()
 
     def run(basis, material, kappa_table):
-        return call(jnp.asarray(matrix, BF16), basis, material, kappa_table)
+        return call(jnp.asarray(matrix, F32), basis, material, kappa_table)
 
     return run

time: 48.7 us -> 40.2 us (0.83)
  Pallas kernels: 42.7 us -> 38 us
  local copies, waits for them, and re-layouts: 5.08 us -> 1.37 us
    pallas_call x1, Pallas kernels: 42.7 us -> 38 us  [shards(): pl.pallas_call(kernel, out_shape=(jax.ShapeDtypeStruct((32, 32), F32), ja...]
    unnamed x9 -> x1, local copies, waits for them, and re-layouts: 4.31 us -> 0.6 us
where the time goes in v2:
time: 40.2 us; the launch traced here: 40 us
  Pallas kernels  38 us (95%)
  local copies, waits for them, and re-layouts  1.37 us (3%)
  between operations  0.64 us (2%)
    pallas_call x1, Pallas kernels, shards(): pl.pallas_call(kernel, out_shape=(jax.ShapeDtypeStruct((32, 32), F32), ja...  38 us

profile of v2, /device:TPU:1, one launch (start us, length us, event | category | flops | bytes accessed | tf_op | source)
XLA Modules:
  0.0 40.0 jit_solution(13126237949110149588)
XLA Ops:
  0.6 38.0 %coarse_blocks.1 = (f32[32,32]{1,0:T(8,128)S(1)}, f32[32,256]{1,0:T(8,128)S(1)}) custom-call(f32[3072,128]{1,0:T(8,128)} %bitcast.9, s32[32,128]{1,0:T(8,128)} %bitcast.11, f32[8]{0:T(128)} %table.1, f32[432,192]{1,0:T(8,128)} %constant.2.clone.stencil), custom_call_target="tpu_custom_call" | custom-call | tf_op jit(solution)/shard_map/coarse_blocks/pallas_call | solution.py:397
  38.7 0.1 reshape.15
  38.8 0.7 %copy.8 = f32[32,8,32]{2,0,1:T(8,128)} copy(f32[32,8,32]{2,1,0:T(8,128)S(1)} %reshape.15) | data formatting | bytes 65536 | tf_op jit(solution)/shard_map/reshape | solution.py:435
  39.4 0.6 %copy.10 = f32[1,32,32]{2,1,0:T(8,128)} copy(f32[1,32,32]{2,1,0:T(8,128)S(1)} %bitcast.8) | data formatting | bytes 8192

commit v3 on v2

--- a/solution.py
+++ b/solution.py
@@ -17,7 +17,9 @@
 GHOSTS = 42
 ROWS = 144
 ALL_NEAR = [(p, r) for p in (-1, 0, 1) for r in (-1, 0, 1) if (p, r) != (0, 0)]
-FORWARD = [(0, 1), (1, -1), (1, 0), (1, 1)]
+UNROLL_E = 4
+UNROLL_S = 2
+UNROLL_N = 2
 
 
 def out_cells():
@@ -71,8 +73,8 @@
 
 def kernel(basis, material, table, stencil, factor, panel,
            zs, mat, c_all, fb, rb, ks, packy, gin, gout, khx, khy, khc, ke, kd, kt, k3,
-           ss, sgk, qb, nin, fin, bout, bin_, tab, c_in,
-           lsem, gs, gr, hs, hr, fs, fr, ns, nr, es, er, bs, br):
+           ss, sgk, qb, qg, qc, nin, inbox, outbox, tab, c_in,
+           lsem, gs, gr, hs, hr, fs, fr, cs, cr, ns, nr, bs, br):
     s = lax.axis_index("sub")
     g = lax.axis_index("grp")
     i = s // YDOMS
@@ -134,9 +136,6 @@
     for x in range(4):
         for a in range(3):
             fb[24 + 3 * x + a] = zs[pl.ds(a * 1024 + x * 8, 32, stride=32), :]
-    for a in range(3):
-        fb[36 + a] = zs[pl.ds(a * 1024 + 7, 32, stride=32), :]
-
     lane24 = lax.broadcasted_iota(jnp.int32, (24, 128), 1)
 
     def own(col):
@@ -154,7 +153,7 @@
         return first, last
 
     zero24 = jnp.zeros((24, 128), F32)
-    first, last = lax.fori_loop(0, 32, edge, (zero24, zero24))
+    first, last = lax.fori_loop(0, 32, edge, (zero24, zero24), unroll=UNROLL_E)
     gout[0, 32:56, :] = first
     gout[1, 32:56, :] = last
 
@@ -178,14 +177,36 @@
     ]
     for copy in halo:
         copy.start()
-    faces = []
-    for a in range(3):
-        faces.append(remote(fb.at[pl.ds(8 * a, 8)], rb.at[pl.ds(8 * a, 8)], fs.at[a], fr.at[a], near(-1, 0), g))
-    faces.append(remote(fb.at[pl.ds(24, 12)], rb.at[pl.ds(24, 12)], fs.at[3], fr.at[3], near(0, -1), g))
-    faces.append(remote(fb.at[pl.ds(24, 3)], rb.at[pl.ds(36, 3)], fs.at[4], fr.at[4], near(-1, -1), g))
-    faces.append(remote(fb.at[pl.ds(36, 3)], rb.at[pl.ds(39, 3)], fs.at[5], fr.at[5], near(-1, 1), g))
-    for copy in faces:
-        copy.start()
+    faces = [
+        (1, 0, remote(fb.at[pl.ds(8 * a, 8)], rb.at[pl.ds(8 * a, 8)], fs.at[a], fr.at[a], near(-1, 0), g))
+        for a in range(3)
+    ]
+    faces.append((0, 1, remote(fb.at[pl.ds(24, 12)], rb.at[pl.ds(24, 12)], fs.at[3], fr.at[3], near(0, -1), g)))
+    for p, r, copy in faces:
+        pl.when(inside(-p, -r))(copy.start)
+
+    kpair = jnp.concatenate([k3[...], k3[...]], axis=1)
+    c_ghost = jnp.concatenate([c_all[part * ROWS + 96 : (part + 1) * ROWS, :] for part in range(3)], axis=0)
+    lane_all = lax.broadcasted_iota(jnp.int32, (ROWS, 128), 1)
+    lane48 = lax.broadcasted_iota(jnp.int32, (48, 128), 1)
+
+    def pair(step, carry):
+        u = jnp.concatenate([own(2 * step), own(2 * step + 1)], axis=1)
+        r = dot(c_all[...], split(u))
+        rk = dot(c_ghost, split(u * kpair))
+        for half in range(2):
+            col = 2 * step + half
+            part = r[:, 128 * half : 128 * half + 128]
+            up = jnp.where(lane_all == 127, 0.0, pltpu.roll(part[ROWS : 2 * ROWS], 127, 1))
+            down = jnp.where(lane_all == 0, 0.0, pltpu.roll(part[2 * ROWS :], 1, 1))
+            ss[pl.ds(pl.multiple_of(col * ROWS, ROWS), ROWS), :] = part[:ROWS] + up + down
+            part = rk[:, 128 * half : 128 * half + 128]
+            up = jnp.where(lane48 == 127, 0.0, pltpu.roll(part[48:96], 127, 1))
+            down = jnp.where(lane48 == 0, 0.0, pltpu.roll(part[96:], 1, 1))
+            sgk[pl.ds(pl.multiple_of(col * 48, 48), 48), :] = part[:48] + up + down
+        return carry
+
+    lax.fori_loop(0, 16, pair, 0, unroll=UNROLL_S)
 
     to_low.wait_recv()
     to_high.wait_recv()
@@ -208,30 +229,6 @@
     kedges = jnp.where(lane96 < 32, h_high * kc_high, pltpu.roll(h_low * kc_low, 32, 1))
     edges = jnp.where(lane96 < 64, edges, pltpu.roll(kedges, 64, 1))
     ch = dot(c_all[...], split(edges))
-    ch_high = ch[ROWS : 2 * ROWS]
-    ch_low = ch[2 * ROWS : 3 * ROWS]
-    lane_all = lax.broadcasted_iota(jnp.int32, (ROWS, 128), 1)
-    lane48 = lax.broadcasted_iota(jnp.int32, (48, 128), 1)
-    kpair = jnp.concatenate([k3[...], k3[...]], axis=1)
-    c_ghost = jnp.concatenate([c_all[part * ROWS + 96 : (part + 1) * ROWS, :] for part in range(3)], axis=0)
-
-    def pair(step, carry):
-        u = jnp.concatenate([own(2 * step), own(2 * step + 1)], axis=1)
-        r = dot(c_all[...], split(u))
-        rk = dot(c_ghost, split(u * kpair))
-        for half in range(2):
-            col = 2 * step + half
-            part = r[:, 128 * half : 128 * half + 128]
-            up = jnp.where(lane_all == 127, pltpu.roll(ch_high, 127 - col, 1), pltpu.roll(part[ROWS : 2 * ROWS], 127, 1))
-            down = jnp.where(lane_all == 0, pltpu.roll(ch_low, 96 - col, 1), pltpu.roll(part[2 * ROWS :], 1, 1))
-            ss[pl.ds(pl.multiple_of(col * ROWS, ROWS), ROWS), :] = part[:ROWS] + up + down
-            part = rk[:, 128 * half : 128 * half + 128]
-            up = jnp.where(lane48 == 127, pltpu.roll(ch_high[96:], 63 - col, 1), pltpu.roll(part[48:96], 127, 1))
-            down = jnp.where(lane48 == 0, pltpu.roll(ch_low[96:], 32 - col, 1), pltpu.roll(part[96:], 1, 1))
-            sgk[pl.ds(pl.multiple_of(col * 48, 48), 48), :] = part[:48] + up + down
-        return carry
-
-    lax.fori_loop(0, 16, pair, 0)
 
     for copy in halo:
         copy.wait_recv()
@@ -259,21 +256,45 @@
         kt[39 + a : 40 + a, :] = khc[2, 0:1, :]
     kt[42:48, :] = jnp.zeros((6, 128), F32)
 
-    near_low = jnp.concatenate([smooth[:, 0:1]] * 3, axis=0) * 18.0
-    near_high = jnp.concatenate([smooth[:, 127:128]] * 3, axis=0) * 18.0
-    layers = jnp.concatenate([h_low, h_high], axis=0)
-    weighted = jnp.concatenate([h_low * near_low, h_high * near_high], axis=0)
-    outside = dot_tn(weighted, layers)[:32, :32]
+    def column(tile, at):
+        return jnp.concatenate([tile[:, at : at + 1]] * 3, axis=0)
+
+    own_low = spread(gout[0, 32:56, :])
+    own_high = spread(gout[1, 32:56, :])
+    left = jnp.concatenate([
+        h_low * (18.0 * column(smooth, 0)), h_high * (18.0 * column(smooth, 127)),
+        -own_high * column(kappa, 127), -own_low * column(kappa, 0)], axis=0)
+    right = jnp.concatenate([
+        h_low, h_high, ch[ROWS : ROWS + 96], pltpu.roll(ch[2 * ROWS : 2 * ROWS + 96], 96, 1)], axis=0)
+    outside = dot_tn(left, right)[:32, :32]
+
+    g_high = ch[ROWS + 96 : 2 * ROWS]
+    g_low = ch[2 * ROWS + 96 :]
+    g_high = kt[:, 127:128] * g_high + pltpu.roll(g_high, 64, 1)
+    g_low = kt[:, 0:1] * g_low + pltpu.roll(g_low, 64, 1)
+    turn = jnp.where(lane48 < 32, g_high, g_low).T
+    turn_high = jnp.concatenate([turn[0:32], jnp.zeros((32, 80), F32)], axis=1)
+    turn_low = jnp.concatenate([turn[32:64], jnp.zeros((32, 80), F32)], axis=1)
 
     def ghost(step, carry):
         tiles = []
         for y in range(8):
             m = step * 8 + y
-            tiles.append(kt[pl.ds(m, 1), :] * ss[pl.ds(96 + m, 32, stride=ROWS), :] + sgk[pl.ds(m, 32, stride=48), :])
+            tile = kt[pl.ds(m, 1), :] * ss[pl.ds(96 + m, 32, stride=ROWS), :] + sgk[pl.ds(m, 32, stride=48), :]
+            high = jnp.where(lane == 127, pltpu.roll(turn_high, 127 - m, 1), 0.0)
+            tile = tile + jnp.where(lane == 0, pltpu.roll(turn_low, lax.rem(128 - m, 128), 1), high)
+            qg[m] = tile
+            tiles.append(tile)
         qb[:, pl.ds(pl.multiple_of(step * 1024, 1024), 1024)] = split(jnp.concatenate(tiles, axis=1))
         return carry
 
     lax.fori_loop(0, 6, ghost, 0)
+    corners = [
+        (0, 1, remote(qg.at[pl.ds(36, 3)], qc.at[0], cs.at[0], cr.at[0], near(0, 1), g)),
+        (0, -1, remote(qg.at[pl.ds(39, 3)], qc.at[1], cs.at[1], cr.at[1], near(0, -1), g)),
+    ]
+    for p, r, copy in corners:
+        pl.when(inside(p, r))(copy.start)
 
     def inner(step, total):
         start_z = (step // 4) * 1024 + lax.rem(step, 4) * 8
@@ -289,62 +310,69 @@
         right = split(jnp.concatenate(right, axis=1))
         return total + dot_nt(left, right)
 
-    total = quadrants(lax.fori_loop(0, 12, inner, jnp.zeros((64, 64), F32))) + outside
+    total = quadrants(lax.fori_loop(0, 12, inner, jnp.zeros((64, 64), F32), unroll=UNROLL_N)) + outside
     total = (total + total.T) * (1.0 / 48.0)
     nin[g, :, 0:32] = total
     sums = [remote(nin.at[g], nin.at[g], ns.at[d - 1], nr.at[d - 1], s, slab(d)) for d in (1, 2, 3)]
     for copy in sums:
         copy.start()
 
-    def coupled(start, count):
-        f = split(jnp.concatenate([rb[start + t] for t in range(count)], axis=1))
-        return dot_nt(qb[:, start * 128 : (start + count) * 128], f)
+    def face(start, count):
+        return split(jnp.concatenate([rb[start + t] for t in range(count)], axis=1))
 
     lane32 = lax.broadcasted_iota(jnp.int32, (32, 128), 1)
     lane8 = lax.broadcasted_iota(jnp.int32, (8, 128), 1)
 
-    def place(parts):
-        result = jnp.zeros((32, 128), F32)
-        for at, block in parts.items():
-            wide = jnp.concatenate([block, jnp.zeros((32, 96), F32)], axis=1)
-            wide = wide if at == 0 else pltpu.roll(wide, 32 * at, 1)
-            result = jnp.where(lane32 // 32 == at, wide, result)
-        return result
-
-    def turned(block):
-        wide = jnp.concatenate([block.T, jnp.zeros((32, 96), F32)], axis=1)
+    def pack(block):
+        wide = jnp.concatenate([block, jnp.zeros((32, 96), F32)], axis=1)
         result = wide[0:8]
         for k in range(1, 4):
             result = jnp.where(lane8 // 32 == k, pltpu.roll(wide[8 * k : 8 * k + 8], 32 * k, 1), result)
         return result
 
+    def scaled(value, ok):
+        return jnp.where(ok, quadrants(value) * (-1.0 / 48.0), 0.0)
+
     sent = []
 
-    def give(which, at, blocks):
-        tile = place(blocks)
-        fin[which, g] = tile
-        for d in (1, 2, 3):
-            copy = remote(fin.at[which, g], fin.at[which, g], es.at[which, d - 1], er.at[which, d - 1], s, slab(d))
+    def give(src, slot, count, sub, which, slabs):
+        for d in slabs:
+            copy = remote(src, inbox.at[g, pl.ds(slot, count)], bs.at[which, d], br.at[which, d], sub, slab(d))
             copy.start()
             sent.append(copy)
-        for b, block in blocks.items():
-            bout[b] = turned(block)
-            for d in range(4):
-                copy = remote(bout.at[b], bin_.at[b, g], bs.at[b, d], br.at[b, d], near(*FORWARD[b]), slab(d))
-                copy.start()
-                sent.append(copy)
-
-    def finished(b, value):
-        return jnp.where(inside(*FORWARD[b]), quadrants(value) * (-1.0 / 48.0), 0.0)
-
-    for which in (3, 4, 5):
-        faces[which].wait_recv()
-    give(0, 0, {0: finished(0, coupled(24, 12)), 1: finished(1, coupled(39, 3)), 3: finished(3, coupled(36, 3))})
+
+    pl.when(inside(0, 1))(faces[3][2].wait_recv)
+    block = scaled(dot_nt(qb[:, 24 * 128 : 36 * 128], face(24, 12)), inside(0, 1))
+    inbox[g, 4] = pack(block)
+    outbox[0] = pack(block.T)
+    give(inbox.at[g, pl.ds(4, 1)], 4, 1, s, 0, (1, 2, 3))
+    give(outbox.at[pl.ds(0, 1)], 3, 1, near(0, 1), 1, range(4))
+
+    for p, r, copy in corners:
+        pl.when(inside(-p, -r))(copy.wait_recv)
+    side = [split(jnp.concatenate([qc[e, a] for a in range(3)], axis=1)) for e in range(2)]
     value = jnp.zeros((64, 64), F32)
+    value_low = jnp.zeros((64, 64), F32)
+    value_high = jnp.zeros((64, 64), F32)
     for a in range(3):
-        faces[a].wait_recv()
-        value = value + coupled(8 * a, 8)
-    give(1, 2, {2: finished(2, value)})
+        pl.when(inside(1, 0))(faces[a][2].wait_recv)
+        f = face(8 * a, 8)
+        value = value + dot_nt(qb[:, a * 1024 : (a + 1) * 1024], f)
+        value_low = value_low + dot_nt(side[0][:, 128 * a : 128 * a + 128], f[:, 0:128])
+        value_high = value_high + dot_nt(side[1][:, 128 * a : 128 * a + 128], f[:, 896:1024])
+    block = scaled(value, inside(1, 0))
+    block_low = scaled(value_low, inside(1, -1))
+    block_high = scaled(value_high, inside(1, 1))
+    outbox[1] = pack(block_low.T)
+    outbox[2] = pack(block.T)
+    outbox[3] = pack(block_high.T)
+    give(outbox.at[pl.ds(1, 3)], 0, 3, near(1, 0), 2, range(4))
+    outbox[4] = pack(block_low)
+    give(outbox.at[pl.ds(4, 1)], 7, 1, near(0, -1), 3, range(4))
+    outbox[5] = pack(block_high)
+    give(outbox.at[pl.ds(5, 1)], 5, 1, near(0, 1), 4, range(4))
+    inbox[g, 6] = pack(block)
+    give(inbox.at[g, pl.ds(6, 1)], 6, 1, s, 5, (1, 2, 3))
 
     for copy in sums:
         copy.wait_recv()
@@ -365,28 +393,31 @@
 
     for copy in sent:
         copy.wait_recv()
-    ahead = jnp.zeros((32, 128), F32)
-    for h in range(SLABS):
-        ahead = ahead + (fin[0, h] + fin[1, h])
-    behind = [jnp.zeros((8, 128), F32)] * 4
-    packed = [bin_[b, 0] + bin_[b, 1] + bin_[b, 2] + bin_[b, 3] for b in range(4)]
-    order = [3, 2, 1, 0]
-    rows = []
-    for k in range(4):
-        result = jnp.zeros((8, 128), F32)
-        for at in range(4):
-            shift = (32 * (at - k)) % 128
-            moved = packed[order[at]] if shift == 0 else pltpu.roll(packed[order[at]], shift, 1)
-            result = jnp.where(lane8 // 32 == at, moved, result)
-        rows.append(result)
-    every = jnp.concatenate([jnp.concatenate(rows, axis=0), ahead], axis=1)
+    packed = [inbox[0, b] + inbox[1, b] + inbox[2, b] + inbox[3, b] for b in range(8)]
+    halves = []
+    for part in range(2):
+        rows = []
+        for k in range(4):
+            result = jnp.zeros((8, 128), F32)
+            for at in range(4):
+                shift = (32 * (at - k)) % 128
+                moved = packed[4 * part + at]
+                moved = moved if shift == 0 else pltpu.roll(moved, shift, 1)
+                result = jnp.where(lane8 // 32 == at, moved, result)
+            rows.append(result)
+        halves.append(jnp.concatenate(rows, axis=0))
+    every = jnp.concatenate(halves, axis=1)
     panel[...] = lax.dot_general(inverse, every, (((1,), (0,)), ((), ())), precision=lax.Precision.HIGHEST,
                                  preferred_element_type=F32)
 
     to_low.wait_send()
     to_high.wait_send()
-    for copy in faces + halo + sums + sent:
+    for copy in halo + sums + sent:
         copy.wait_send()
+    for p, r, copy in faces:
+        pl.when(inside(-p, -r))(copy.wait_send)
+    for p, r, copy in corners:
+        pl.when(inside(p, r))(copy.wait_send)
 
 
 def shards(stencil, basis, material, kappa_table):
@@ -403,8 +434,8 @@
             pltpu.VMEM((3072, 128), F32),
             pltpu.VMEM((32, 128), jnp.int32),
             pltpu.VMEM((3 * ROWS, 192), BF16),
-            pltpu.VMEM((39, 32, 128), F32),
-            pltpu.VMEM((42, 32, 128), F32),
+            pltpu.VMEM((36, 32, 128), F32),
+            pltpu.VMEM((36, 32, 128), F32),
             pltpu.VMEM((32, 128), F32),
             pltpu.VMEM((2, 8, 128), F32),
             pltpu.VMEM((2, 56, 128), F32),
@@ -419,14 +450,15 @@
             pltpu.VMEM((32 * ROWS, 128), F32),
             pltpu.VMEM((32 * 48, 128), F32),
             pltpu.VMEM((64, 6 * 1024), BF16),
+            pltpu.VMEM((48, 32, 128), F32),
+            pltpu.VMEM((2, 3, 32, 128), F32),
             pltpu.VMEM((4, 32, 128), F32),
-            pltpu.VMEM((2, 4, 32, 128), F32),
-            pltpu.VMEM((4, 8, 128), F32),
-            pltpu.VMEM((4, 4, 8, 128), F32),
+            pltpu.VMEM((4, 8, 8, 128), F32),
+            pltpu.VMEM((6, 8, 128), F32),
             pltpu.SMEM((8,), F32),
             pltpu.VMEM((3 * ROWS, 192), F32),
-            dma((4,)), dma((2,)), dma((2,)), dma((8,)), dma((8,)), dma((6,)), dma((6,)),
-            dma((3,)), dma((3,)), dma((2, 3)), dma((2, 3)), dma((4, 4)), dma((4, 4)),
+            dma((4,)), dma((2,)), dma((2,)), dma((8,)), dma((8,)), dma((4,)), dma((4,)), dma((2,)), dma((2,)),
+            dma((3,)), dma((3,)), dma((6, 4)), dma((6, 4)),
         ],
         compiler_params=pltpu.CompilerParams(
             collective_id=0, has_side_effects=True, vmem_limit_bytes=40 * 2**20),

time: 40.2 us -> 34.9 us (0.87)
  Pallas kernels: 38 us -> 32.8 us
    pallas_call x1, Pallas kernels: 38 us -> 32.8 us  [shards(): pl.pallas_call(kernel, out_shape=(jax.ShapeDtypeStruct((32, 32), F32), ja...]
where the time goes in v3:
time: 34.9 us; the launch traced here: 34.8 us
  Pallas kernels  32.8 us (94%)
  local copies, waits for them, and re-layouts  1.37 us (4%)
  between operations  0.64 us (2%)
    pallas_call x1, Pallas kernels, shards(): pl.pallas_call(kernel, out_shape=(jax.ShapeDtypeStruct((32, 32), F32), ja...  32.8 us
    reshape x2, local copies, waits for them, and re-layouts, shards(): panel = panel.reshape(32, 8, 32).transpose(1, 0, 2)  0.77 us

profile of v3, /device:TPU:1, one launch (start us, length us, event | category | flops | bytes accessed | tf_op | source)
XLA Modules:
  0.0 34.8 jit_solution(1004104866031490890)
XLA Ops:
  0.6 32.8 %coarse_blocks.1 = (f32[32,32]{1,0:T(8,128)S(1)}, f32[32,256]{1,0:T(8,128)S(1)}) custom-call(f32[3072,128]{1,0:T(8,128)} %bitcast.9, s32[32,128]{1,0:T(8,128)} %bitcast.11, f32[8]{0:T(128)} %table.1, f32[432,192]{1,0:T(8,128)} %constant.2.clone.stencil), custom_call_target="tpu_custom_call" | custom-call | tf_op jit(solution)/shard_map/coarse_blocks/pallas_call | solution.py:428
  33.4 0.1 reshape.15
  33.5 0.7 %copy.8 = f32[32,8,32]{2,0,1:T(8,128)} copy(f32[32,8,32]{2,1,0:T(8,128)S(1)} %reshape.15) | data formatting | bytes 65536 | tf_op jit(solution)/shard_map/reshape | solution.py:467
  34.2 0.6 %copy.10 = f32[1,32,32]{2,1,0:T(8,128)} copy(f32[1,32,32]{2,1,0:T(8,128)S(1)} %bitcast.8) | data formatting | bytes 8192

commit v4 on v3

--- a/solution.py
+++ b/solution.py
@@ -17,7 +17,7 @@
 GHOSTS = 42
 ROWS = 144
 ALL_NEAR = [(p, r) for p in (-1, 0, 1) for r in (-1, 0, 1) if (p, r) != (0, 0)]
-UNROLL_E = 4
+UNROLL_E = 8
 UNROLL_S = 2
 UNROLL_N = 2
 
@@ -71,10 +71,10 @@
     return top[:, :32] + top[:, 32:]
 
 
-def kernel(basis, material, table, stencil, factor, panel,
-           zs, mat, c_all, fb, rb, ks, packy, gin, gout, khx, khy, khc, ke, kd, kt, k3,
+def kernel(basis, planes, material, table, stencil, factor, panel,
+           zs, mat, c_all, fb, rx, ry, ks, packy, gin, gout, khx, khy, khc, ke, kd, kt, k3,
            ss, sgk, qb, qg, qc, nin, inbox, outbox, tab, c_in,
-           lsem, gs, gr, hs, hr, fs, fr, cs, cr, ns, nr, bs, br):
+           hello, ready, lsem, gs, gr, hs, hr, fs, fr, cs, cr, ns, nr, bs, br):
     s = lax.axis_index("sub")
     g = lax.axis_index("grp")
     i = s // YDOMS
@@ -84,7 +84,7 @@
         return lax.rem(i + p + XDOMS, XDOMS) * YDOMS + lax.rem(j + r + YDOMS, YDOMS)
 
     def inside(p, r):
-        ok = jnp.bool_(True)
+        ok = i >= 0
         if p:
             ok = jnp.logical_and(ok, i < XDOMS - 1 if p > 0 else i > 0)
         if r:
@@ -100,10 +100,19 @@
             device_id={"sub": sub, "grp": grp}, device_id_type=MESH)
 
     barrier = pltpu.get_barrier_semaphore()
+    entered = g
     for p, r in ALL_NEAR:
-        pl.semaphore_signal(barrier, inc=1, device_id={"sub": near(p, r), "grp": g}, device_id_type=MESH)
+        entered = entered + inside(p, r).astype(jnp.int32)
+
+        @pl.when(inside(p, r))
+        def _():
+            pl.semaphore_signal(barrier, inc=1, device_id={"sub": near(p, r), "grp": g}, device_id_type=MESH)
+
     for d in (1, 2, 3):
-        pl.semaphore_signal(barrier, inc=1, device_id={"sub": s, "grp": slab(d)}, device_id_type=MESH)
+
+        @pl.when(g + d < SLABS)
+        def _():
+            pl.semaphore_signal(barrier, inc=1, device_id={"sub": s, "grp": slab(d)}, device_id_type=MESH)
 
     load_mat = pltpu.make_async_copy(material, mat, lsem.at[0])
     load_zs = pltpu.make_async_copy(basis, zs, lsem.at[1])
@@ -130,12 +139,35 @@
     gout[1, 0:32, :] = kappa
 
     load_zs.wait()
-    for a in range(3):
-        for y in range(8):
-            fb[8 * a + y] = zs[pl.ds(a * 1024 + y, 32, stride=32), :]
     for x in range(4):
         for a in range(3):
-            fb[24 + 3 * x + a] = zs[pl.ds(a * 1024 + x * 8, 32, stride=32), :]
+            fb[3 * x + a] = zs[pl.ds(a * 1024 + x * 8, 32, stride=32), :]
+    pl.semaphore_wait(barrier, entered)
+    for d in (1, 2, 3):
+
+        @pl.when(g >= d)
+        def _():
+            pl.semaphore_signal(hello.at[min(d, 2) - 1], inc=1, device_id={"sub": s, "grp": slab(-d)}, device_id_type=MESH)
+
+    halo = [
+        (-1, 0, remote(ks.at[pl.ds(0, 8)], khx.at[1], hs.at[0], hr.at[0], near(-1, 0), g)),
+        (1, 0, remote(ks.at[pl.ds(24, 8)], khx.at[0], hs.at[1], hr.at[1], near(1, 0), g)),
+        (0, -1, remote(packy.at[0], khy.at[1], hs.at[2], hr.at[2], near(0, -1), g)),
+        (0, 1, remote(packy.at[1], khy.at[0], hs.at[3], hr.at[3], near(0, 1), g)),
+        (-1, -1, remote(packy.at[0], khc.at[3], hs.at[4], hr.at[4], near(-1, -1), g)),
+        (1, 1, remote(packy.at[1], khc.at[0], hs.at[5], hr.at[5], near(1, 1), g)),
+        (-1, 1, remote(packy.at[1], khc.at[2], hs.at[6], hr.at[6], near(-1, 1), g)),
+        (1, -1, remote(packy.at[0], khc.at[1], hs.at[7], hr.at[7], near(1, -1), g)),
+    ]
+    for p, r, copy in halo:
+        pl.when(inside(p, r))(copy.start)
+    faces = [
+        (1, 0, remote(planes.at[pl.ds(32 * a, 32), pl.ds(0, 8)], rx.at[pl.ds(32 * a, 32)], fs.at[a], fr.at[a], near(-1, 0), g))
+        for a in range(3)
+    ]
+    faces.append((0, 1, remote(fb, ry, fs.at[3], fr.at[3], near(0, -1), g)))
+    for p, r, copy in faces[:1]:
+        pl.when(inside(-p, -r))(copy.start)
     lane24 = lax.broadcasted_iota(jnp.int32, (24, 128), 1)
 
     def own(col):
@@ -157,34 +189,21 @@
     gout[0, 32:56, :] = first
     gout[1, 32:56, :] = last
 
+    to_low = remote(gout.at[0], gin.at[1], gs.at[0], gr.at[1], s, slab(-1))
+    to_high = remote(gout.at[1], gin.at[0], gs.at[1], gr.at[0], s, slab(1))
+    low_ok = g > 0
+    high_ok = g < SLABS - 1
+    pl.when(low_ok)(to_low.start)
+
+    @pl.when(high_ok)
+    def _():
+        pl.semaphore_wait(hello.at[0], 1)
+        to_high.start()
+
+    for p, r, copy in faces[1:]:
+        pl.when(inside(-p, -r))(copy.start)
     load_c.wait()
     c_all[...] = c_in[...].astype(BF16)
-    pl.semaphore_wait(barrier, len(ALL_NEAR) + 3)
-
-    to_low = remote(gout.at[0], gin.at[1], gs.at[0], gr.at[1], s, slab(-1))
-    to_high = remote(gout.at[1], gin.at[0], gs.at[1], gr.at[0], s, slab(1))
-    to_low.start()
-    to_high.start()
-    halo = [
-        remote(ks.at[pl.ds(0, 8)], khx.at[1], hs.at[0], hr.at[0], near(-1, 0), g),
-        remote(ks.at[pl.ds(24, 8)], khx.at[0], hs.at[1], hr.at[1], near(1, 0), g),
-        remote(packy.at[0], khy.at[1], hs.at[2], hr.at[2], near(0, -1), g),
-        remote(packy.at[1], khy.at[0], hs.at[3], hr.at[3], near(0, 1), g),
-        remote(packy.at[0], khc.at[3], hs.at[4], hr.at[4], near(-1, -1), g),
-        remote(packy.at[1], khc.at[0], hs.at[5], hr.at[5], near(1, 1), g),
-        remote(packy.at[1], khc.at[2], hs.at[6], hr.at[6], near(-1, 1), g),
-        remote(packy.at[0], khc.at[1], hs.at[7], hr.at[7], near(1, -1), g),
-    ]
-    for copy in halo:
-        copy.start()
-    faces = [
-        (1, 0, remote(fb.at[pl.ds(8 * a, 8)], rb.at[pl.ds(8 * a, 8)], fs.at[a], fr.at[a], near(-1, 0), g))
-        for a in range(3)
-    ]
-    faces.append((0, 1, remote(fb.at[pl.ds(24, 12)], rb.at[pl.ds(24, 12)], fs.at[3], fr.at[3], near(0, -1), g)))
-    for p, r, copy in faces:
-        pl.when(inside(-p, -r))(copy.start)
-
     kpair = jnp.concatenate([k3[...], k3[...]], axis=1)
     c_ghost = jnp.concatenate([c_all[part * ROWS + 96 : (part + 1) * ROWS, :] for part in range(3)], axis=0)
     lane_all = lax.broadcasted_iota(jnp.int32, (ROWS, 128), 1)
@@ -208,11 +227,9 @@
 
     lax.fori_loop(0, 16, pair, 0, unroll=UNROLL_S)
 
-    to_low.wait_recv()
-    to_high.wait_recv()
+    pl.when(high_ok)(to_low.wait_recv)
+    pl.when(low_ok)(to_high.wait_recv)
     lane = lax.broadcasted_iota(jnp.int32, (32, 128), 1)
-    low_ok = g > 0
-    high_ok = g < SLABS - 1
     k_low = jnp.where(low_ok, gin[0, 0:32, :], 0.0)
     k_high = jnp.where(high_ok, gin[1, 0:32, :], 0.0)
     lane96 = lax.broadcasted_iota(jnp.int32, (96, 128), 1)
@@ -230,8 +247,8 @@
     edges = jnp.where(lane96 < 64, edges, pltpu.roll(kedges, 64, 1))
     ch = dot(c_all[...], split(edges))
 
-    for copy in halo:
-        copy.wait_recv()
+    for p, r, copy in halo:
+        pl.when(inside(-p, -r))(copy.wait_recv)
     ke[...] = jnp.zeros_like(ke)
     for x in range(4):
         ke[1 + x, 1:9, :] = ks[8 * x : 8 * x + 8, :]
@@ -243,8 +260,8 @@
     ke[0, 9:10, :] = jnp.where(inside(-1, 1), khc[1, 3:4, :], 0.0)
     ke[5, 0:1, :] = jnp.where(inside(1, -1), khc[2, 0:1, :], 0.0)
     ke[5, 9:10, :] = jnp.where(inside(1, 1), khc[3, 0:1, :], 0.0)
-    planes = [ke[x, 1:9, :] + 0.5 * (ke[x, 0:8, :] + ke[x, 2:10, :]) for x in range(6)]
-    smooth = jnp.concatenate([planes[x + 1] + 0.5 * (planes[x] + planes[x + 2]) for x in range(4)], axis=0)
+    strips = [ke[x, 1:9, :] + 0.5 * (ke[x, 0:8, :] + ke[x, 2:10, :]) for x in range(6)]
+    smooth = jnp.concatenate([strips[x + 1] + 0.5 * (strips[x] + strips[x + 2]) for x in range(4)], axis=0)
     up = jnp.where(lane == 127, 0.0, pltpu.roll(smooth, 127, 1))
     down = jnp.where(lane == 0, 0.0, pltpu.roll(smooth, 1, 1))
     kd[...] = 228.0 * ks[...] + 36.0 * smooth + 18.0 * (up + down)
@@ -295,6 +312,18 @@
     ]
     for p, r, copy in corners:
         pl.when(inside(p, r))(copy.start)
+
+    @pl.when(g < SLABS - 2)
+    def _():
+        pl.semaphore_wait(hello.at[1], SLABS - 2 - g)
+
+    heard = jnp.int32(0)
+    for p, r in ((1, 0), (0, 1), (0, -1)):
+        heard = heard + inside(p, r).astype(jnp.int32)
+
+        @pl.when(inside(-p, -r))
+        def _():
+            pl.semaphore_signal(ready, inc=1, device_id={"sub": near(-p, -r), "grp": g}, device_id_type=MESH)
 
     def inner(step, total):
         start_z = (step // 4) * 1024 + lax.rem(step, 4) * 8
@@ -317,8 +346,10 @@
     for copy in sums:
         copy.start()
 
-    def face(start, count):
-        return split(jnp.concatenate([rb[start + t] for t in range(count)], axis=1))
+    flat = rx.reshape(768, 128)
+
+    def face(a):
+        return split(jnp.concatenate([flat[pl.ds(a * 256 + y, 32, stride=8), :] for y in range(8)], axis=1))
 
     lane32 = lax.broadcasted_iota(jnp.int32, (32, 128), 1)
     lane8 = lax.broadcasted_iota(jnp.int32, (8, 128), 1)
@@ -335,18 +366,20 @@
 
     sent = []
 
-    def give(src, slot, count, sub, which, slabs):
+    def give(src, slot, count, p, r, which, slabs):
         for d in slabs:
-            copy = remote(src, inbox.at[g, pl.ds(slot, count)], bs.at[which, d], br.at[which, d], sub, slab(d))
-            copy.start()
-            sent.append(copy)
+            copy = remote(src, inbox.at[g, pl.ds(slot, count)], bs.at[which, d], br.at[which, d], near(p, r), slab(d))
+            pl.when(inside(p, r))(copy.start)
+            sent.append((p, r, copy))
+
+    pl.semaphore_wait(ready, heard)
 
     pl.when(inside(0, 1))(faces[3][2].wait_recv)
-    block = scaled(dot_nt(qb[:, 24 * 128 : 36 * 128], face(24, 12)), inside(0, 1))
+    block = scaled(dot_nt(qb[:, 24 * 128 : 36 * 128], split(jnp.concatenate([ry[t] for t in range(12)], axis=1))), inside(0, 1))
     inbox[g, 4] = pack(block)
     outbox[0] = pack(block.T)
-    give(inbox.at[g, pl.ds(4, 1)], 4, 1, s, 0, (1, 2, 3))
-    give(outbox.at[pl.ds(0, 1)], 3, 1, near(0, 1), 1, range(4))
+    give(inbox.at[g, pl.ds(4, 1)], 4, 1, 0, 0, 0, (1, 2, 3))
+    give(outbox.at[pl.ds(0, 1)], 3, 1, 0, 1, 1, range(4))
 
     for p, r, copy in corners:
         pl.when(inside(-p, -r))(copy.wait_recv)
@@ -356,7 +389,7 @@
     value_high = jnp.zeros((64, 64), F32)
     for a in range(3):
         pl.when(inside(1, 0))(faces[a][2].wait_recv)
-        f = face(8 * a, 8)
+        f = face(a)
         value = value + dot_nt(qb[:, a * 1024 : (a + 1) * 1024], f)
         value_low = value_low + dot_nt(side[0][:, 128 * a : 128 * a + 128], f[:, 0:128])
         value_high = value_high + dot_nt(side[1][:, 128 * a : 128 * a + 128], f[:, 896:1024])
@@ -366,13 +399,13 @@
     outbox[1] = pack(block_low.T)
     outbox[2] = pack(block.T)
     outbox[3] = pack(block_high.T)
-    give(outbox.at[pl.ds(1, 3)], 0, 3, near(1, 0), 2, range(4))
+    give(outbox.at[pl.ds(1, 3)], 0, 3, 1, 0, 2, range(4))
     outbox[4] = pack(block_low)
-    give(outbox.at[pl.ds(4, 1)], 7, 1, near(0, -1), 3, range(4))
+    give(outbox.at[pl.ds(4, 1)], 7, 1, 0, -1, 3, range(4))
     outbox[5] = pack(block_high)
-    give(outbox.at[pl.ds(5, 1)], 5, 1, near(0, 1), 4, range(4))
+    give(outbox.at[pl.ds(5, 1)], 5, 1, 0, 1, 4, range(4))
     inbox[g, 6] = pack(block)
-    give(inbox.at[g, pl.ds(6, 1)], 6, 1, s, 5, (1, 2, 3))
+    give(inbox.at[g, pl.ds(6, 1)], 6, 1, 0, 0, 5, (1, 2, 3))
 
     for copy in sums:
         copy.wait_recv()
@@ -391,9 +424,9 @@
     factor[...] = lower[:, 0:32] * (1.0 / np.sqrt(49152.0))
     inverse = m[:, 32:64]
 
-    for copy in sent:
-        copy.wait_recv()
-    packed = [inbox[0, b] + inbox[1, b] + inbox[2, b] + inbox[3, b] for b in range(8)]
+    for p, r, copy in sent:
+        pl.when(inside(-p, -r))(copy.wait_recv)
+    packed = [jnp.where(inside(*ALL_NEAR[b]), inbox[0, b] + inbox[1, b] + inbox[2, b] + inbox[3, b], 0.0) for b in range(8)]
     halves = []
     for part in range(2):
         rows = []
@@ -410,10 +443,12 @@
     panel[...] = lax.dot_general(inverse, every, (((1,), (0,)), ((), ())), precision=lax.Precision.HIGHEST,
                                  preferred_element_type=F32)
 
-    to_low.wait_send()
-    to_high.wait_send()
-    for copy in halo + sums + sent:
+    pl.when(low_ok)(to_low.wait_send)
+    pl.when(high_ok)(to_high.wait_send)
+    for copy in sums:
         copy.wait_send()
+    for p, r, copy in halo + sent:
+        pl.when(inside(p, r))(copy.wait_send)
     for p, r, copy in faces:
         pl.when(inside(-p, -r))(copy.wait_send)
     for p, r, copy in corners:
@@ -424,18 +459,19 @@
     hbm = pl.BlockSpec(memory_space=pltpu.HBM)
     vmem = pl.BlockSpec(memory_space=pltpu.VMEM)
     dma = pltpu.SemaphoreType.DMA
-    operands = (basis.reshape(3072, 128), material.reshape(32, 128), kappa_table, stencil)
+    operands = (basis.reshape(3072, 128), basis.reshape(96, 32, 128), material.reshape(32, 128), kappa_table, stencil)
     factor, panel = pl.pallas_call(
         kernel,
         out_shape=(jax.ShapeDtypeStruct((32, 32), F32), jax.ShapeDtypeStruct((32, 256), F32)),
-        in_specs=[hbm, hbm, hbm, hbm],
+        in_specs=[hbm] * 5,
         out_specs=(vmem, vmem),
         scratch_shapes=[
             pltpu.VMEM((3072, 128), F32),
             pltpu.VMEM((32, 128), jnp.int32),
             pltpu.VMEM((3 * ROWS, 192), BF16),
-            pltpu.VMEM((36, 32, 128), F32),
-            pltpu.VMEM((36, 32, 128), F32),
+            pltpu.VMEM((12, 32, 128), F32),
+            pltpu.VMEM((96, 8, 128), F32),
+            pltpu.VMEM((12, 32, 128), F32),
             pltpu.VMEM((32, 128), F32),
             pltpu.VMEM((2, 8, 128), F32),
             pltpu.VMEM((2, 56, 128), F32),
@@ -457,6 +493,7 @@
             pltpu.VMEM((6, 8, 128), F32),
             pltpu.SMEM((8,), F32),
             pltpu.VMEM((3 * ROWS, 192), F32),
+            pltpu.SemaphoreType.REGULAR((2,)), pltpu.SemaphoreType.REGULAR,
             dma((4,)), dma((2,)), dma((2,)), dma((8,)), dma((8,)), dma((4,)), dma((4,)), dma((2,)), dma((2,)),
             dma((3,)), dma((3,)), dma((6, 4)), dma((6, 4)),
         ],

time: 34.9 us -> 32.9 us (0.943)
  the two profiles are of different devices: /device:TPU:1 before, /device:TPU:6 now
where the time goes in v4:
time: 32.9 us; the launch traced here: 32.7 us
  Pallas kernels  30.7 us (93%)
  local copies, waits for them, and re-layouts  1.37 us (4%)
  between operations  0.65 us (2%)
    pallas_call x1, Pallas kernels, shards(): pl.pallas_call(kernel, out_shape=(jax.ShapeDtypeStruct((32, 32), F32), ja...  30.7 us
    reshape x2, local copies, waits for them, and re-layouts, shards(): panel = panel.reshape(32, 8, 32).transpose(1, 0, 2)  0.77 us

profile of v4, /device:TPU:6, one launch (start us, length us, event | category | flops | bytes accessed | tf_op | source)
XLA Modules:
  0.0 32.7 jit_solution(8256769983956789681)
XLA Ops:
  0.6 30.7 %coarse_blocks.1 = (f32[32,32]{1,0:T(8,128)S(1)}, f32[32,256]{1,0:T(8,128)S(1)}) custom-call(f32[3072,128]{1,0:T(8,128)} %bitcast.10, f32[96,32,128]{2,1,0:T(8,128)} %bitcast.11, s32[32,128]{1,0:T(8,128)} %bitcast.13, f32[8]{0:T(128)} %table.1, f32[432,192]{1,0:T(8,128)} %constant.2.clone.stencil), custom_call_target="tpu_custom_call" | custom-call | tf_op jit(solution)/shard_map/coarse_blocks/pallas_call | solution.py:463
  31.3 0.1 reshape.19
  31.4 0.7 %copy.8 = f32[32,8,32]{2,0,1:T(8,128)} copy(f32[32,8,32]{2,1,0:T(8,128)S(1)} %reshape.19) | data formatting | bytes 65536 | tf_op jit(solution)/shard_map/reshape | solution.py:504
  32.1 0.6 %copy.10 = f32[1,32,32]{2,1,0:T(8,128)} copy(f32[1,32,32]{2,1,0:T(8,128)S(1)} %bitcast.9) | data formatting | bytes 8192

commit v5 on v4

--- a/solution.py
+++ b/solution.py
@@ -135,8 +135,20 @@
             packy[e, x : x + 1, :] = ks[8 * x + y : 8 * x + y + 1, :]
     for a in range(3):
         k3[32 * a : 32 * a + 32, :] = kappa
-    gout[0, 0:32, :] = kappa
-    gout[1, 0:32, :] = kappa
+    lane8 = lax.broadcasted_iota(jnp.int32, (8, 128), 1)
+
+    def fold(wide):
+        result = wide[0:8]
+        for k in range(1, 4):
+            result = jnp.where(lane8 // 32 == k, pltpu.roll(wide[8 * k : 8 * k + 8], 32 * k, 1), result)
+        return result
+
+    def spread(packed):
+        return jnp.concatenate(
+            [packed if k == 0 else pltpu.roll(packed, 128 - 32 * k, 1) for k in range(4)], axis=0)
+
+    gout[0, 0:8, :] = fold(kappa)
+    gout[1, 0:8, :] = fold(pltpu.roll(kappa, 1, 1))
 
     load_zs.wait()
     for x in range(4):
@@ -166,7 +178,7 @@
         for a in range(3)
     ]
     faces.append((0, 1, remote(fb, ry, fs.at[3], fr.at[3], near(0, -1), g)))
-    for p, r, copy in faces[:1]:
+    for p, r, copy in faces[3:] + faces[:1]:
         pl.when(inside(-p, -r))(copy.start)
     lane24 = lax.broadcasted_iota(jnp.int32, (24, 128), 1)
 
@@ -186,8 +198,8 @@
 
     zero24 = jnp.zeros((24, 128), F32)
     first, last = lax.fori_loop(0, 32, edge, (zero24, zero24), unroll=UNROLL_E)
-    gout[0, 32:56, :] = first
-    gout[1, 32:56, :] = last
+    gout[0, 8:32, :] = first
+    gout[1, 8:32, :] = last
 
     to_low = remote(gout.at[0], gin.at[1], gs.at[0], gr.at[1], s, slab(-1))
     to_high = remote(gout.at[1], gin.at[0], gs.at[1], gr.at[0], s, slab(1))
@@ -200,7 +212,7 @@
         pl.semaphore_wait(hello.at[0], 1)
         to_high.start()
 
-    for p, r, copy in faces[1:]:
+    for p, r, copy in faces[1:3]:
         pl.when(inside(-p, -r))(copy.start)
     load_c.wait()
     c_all[...] = c_in[...].astype(BF16)
@@ -230,18 +242,12 @@
     pl.when(high_ok)(to_low.wait_recv)
     pl.when(low_ok)(to_high.wait_recv)
     lane = lax.broadcasted_iota(jnp.int32, (32, 128), 1)
-    k_low = jnp.where(low_ok, gin[0, 0:32, :], 0.0)
-    k_high = jnp.where(high_ok, gin[1, 0:32, :], 0.0)
     lane96 = lax.broadcasted_iota(jnp.int32, (96, 128), 1)
 
-    def spread(packed):
-        return jnp.concatenate(
-            [packed if k == 0 else pltpu.roll(packed, 128 - 32 * k, 1) for k in range(4)], axis=0)
-
-    h_high = spread(jnp.where(high_ok, gin[1, 32:56, :], 0.0))
-    h_low = spread(jnp.where(low_ok, gin[0, 32:56, :], 0.0))
-    kc_high = jnp.concatenate([k_high[:, 0:1]] * 3, axis=0)
-    kc_low = jnp.concatenate([k_low[:, 127:128]] * 3, axis=0)
+    h_high = spread(jnp.where(high_ok, gin[1, 8:32, :], 0.0))
+    h_low = spread(jnp.where(low_ok, gin[0, 8:32, :], 0.0))
+    kc_high = jnp.concatenate([spread(jnp.where(high_ok, gin[1, 0:8, :], 0.0))[:, 0:1]] * 3, axis=0)
+    kc_low = jnp.concatenate([spread(jnp.where(low_ok, gin[0, 0:8, :], 0.0))[:, 0:1]] * 3, axis=0)
     edges = jnp.where(lane96 < 32, h_high, pltpu.roll(h_low, 32, 1))
     kedges = jnp.where(lane96 < 32, h_high * kc_high, pltpu.roll(h_low * kc_low, 32, 1))
     edges = jnp.where(lane96 < 64, edges, pltpu.roll(kedges, 64, 1))
@@ -276,8 +282,8 @@
     def column(tile, at):
         return jnp.concatenate([tile[:, at : at + 1]] * 3, axis=0)
 
-    own_low = spread(gout[0, 32:56, :])
-    own_high = spread(gout[1, 32:56, :])
+    own_low = spread(gout[0, 8:32, :])
+    own_high = spread(gout[1, 8:32, :])
     left = jnp.concatenate([
         h_low * (18.0 * column(smooth, 0)), h_high * (18.0 * column(smooth, 127)),
         -own_high * column(kappa, 127), -own_low * column(kappa, 0)], axis=0)
@@ -352,14 +358,8 @@
         return split(jnp.concatenate([flat[pl.ds(a * 256 + y, 32, stride=8), :] for y in range(8)], axis=1))
 
     lane32 = lax.broadcasted_iota(jnp.int32, (32, 128), 1)
-    lane8 = lax.broadcasted_iota(jnp.int32, (8, 128), 1)
-
     def pack(block):
-        wide = jnp.concatenate([block, jnp.zeros((32, 96), F32)], axis=1)
-        result = wide[0:8]
-        for k in range(1, 4):
-            result = jnp.where(lane8 // 32 == k, pltpu.roll(wide[8 * k : 8 * k + 8], 32 * k, 1), result)
-        return result
+        return fold(jnp.concatenate([block, jnp.zeros((32, 96), F32)], axis=1))
 
     def scaled(value, ok):
         return jnp.where(ok, quadrants(value) * (-1.0 / 48.0), 0.0)
@@ -396,16 +396,16 @@
     block = scaled(value, inside(1, 0))
     block_low = scaled(value_low, inside(1, -1))
     block_high = scaled(value_high, inside(1, 1))
+    inbox[g, 6] = pack(block)
     outbox[1] = pack(block_low.T)
     outbox[2] = pack(block.T)
     outbox[3] = pack(block_high.T)
-    give(outbox.at[pl.ds(1, 3)], 0, 3, 1, 0, 2, range(4))
     outbox[4] = pack(block_low)
-    give(outbox.at[pl.ds(4, 1)], 7, 1, 0, -1, 3, range(4))
     outbox[5] = pack(block_high)
-    give(outbox.at[pl.ds(5, 1)], 5, 1, 0, 1, 4, range(4))
-    inbox[g, 6] = pack(block)
-    give(inbox.at[g, pl.ds(6, 1)], 6, 1, 0, 0, 5, (1, 2, 3))
+    give(outbox.at[pl.ds(1, 3)], 0, 3, 1, 0, 2, (2, 3, 1, 0))
+    give(inbox.at[g, pl.ds(6, 1)], 6, 1, 0, 0, 5, (2, 3, 1))
+    give(outbox.at[pl.ds(4, 1)], 7, 1, 0, -1, 3, (2, 3, 1, 0))
+    give(outbox.at[pl.ds(5, 1)], 5, 1, 0, 1, 4, (2, 3, 1, 0))
 
     for copy in sums:
         copy.wait_recv()
@@ -440,8 +440,10 @@
             rows.append(result)
         halves.append(jnp.concatenate(rows, axis=0))
     every = jnp.concatenate(halves, axis=1)
-    panel[...] = lax.dot_general(inverse, every, (((1,), (0,)), ((), ())), precision=lax.Precision.HIGHEST,
-                                 preferred_element_type=F32)
+    solved = lax.dot_general(inverse, every, (((1,), (0,)), ((), ())), precision=lax.Precision.HIGHEST,
+                             preferred_element_type=F32)
+    for b in range(8):
+        panel[b] = solved[:, 32 * b : 32 * b + 32]
 
     pl.when(low_ok)(to_low.wait_send)
     pl.when(high_ok)(to_high.wait_send)
@@ -462,7 +464,7 @@
     operands = (basis.reshape(3072, 128), basis.reshape(96, 32, 128), material.reshape(32, 128), kappa_table, stencil)
     factor, panel = pl.pallas_call(
         kernel,
-        out_shape=(jax.ShapeDtypeStruct((32, 32), F32), jax.ShapeDtypeStruct((32, 256), F32)),
+        out_shape=(jax.ShapeDtypeStruct((32, 32), F32), jax.ShapeDtypeStruct((8, 32, 32), F32)),
         in_specs=[hbm] * 5,
         out_specs=(vmem, vmem),
         scratch_shapes=[
@@ -474,8 +476,8 @@
             pltpu.VMEM((12, 32, 128), F32),
             pltpu.VMEM((32, 128), F32),
             pltpu.VMEM((2, 8, 128), F32),
-            pltpu.VMEM((2, 56, 128), F32),
-            pltpu.VMEM((2, 56, 128), F32),
+            pltpu.VMEM((2, 32, 128), F32),
+            pltpu.VMEM((2, 32, 128), F32),
             pltpu.VMEM((2, 8, 128), F32),
             pltpu.VMEM((2, 8, 128), F32),
             pltpu.VMEM((4, 8, 128), F32),
@@ -501,7 +503,6 @@
             collective_id=0, has_side_effects=True, vmem_limit_bytes=40 * 2**20),
         name="coarse_blocks",
     )(*(pltpu.with_memory_space_constraint(value, pltpu.HBM) for value in operands))
-    panel = panel.reshape(32, 8, 32).transpose(1, 0, 2)
     return factor[None], panel[None]
 
 

time: 32.9 us -> 32 us (0.973)
  Pallas kernels: 30.7 us -> 29.6 us
    pallas_call x1, Pallas kernels: 30.7 us -> 29.6 us  [shards(): pl.pallas_call(kernel, out_shape=(jax.ShapeDtypeStruct((32, 32), F32), ja...]
    reshape x2 -> x0, local copies, waits for them, and re-layouts: 0.77 us -> none  [shards(): panel = panel.reshape(32, 8, 32).transpose(1, 0, 2)]
    unnamed x1 -> x2, local copies, waits for them, and re-layouts: 0.6 us -> 1.26 us
where the time goes in v5:
time: 32 us; the launch traced here: 31.5 us
  Pallas kernels  29.6 us (92%)
  local copies, waits for them, and re-layouts  1.26 us (4%)
  between operations  0.64 us (2%)
    pallas_call x1, Pallas kernels, shards(): pl.pallas_call(kernel, out_shape=(jax.ShapeDtypeStruct((32, 32), F32), ja...  29.6 us
    unnamed x2, local copies, waits for them, and re-layouts  1.26 us

profile of v5, /device:TPU:6, one launch (start us, length us, event | category | flops | bytes accessed | tf_op | source)
XLA Modules:
  0.0 31.5 jit_solution(11375518472005444181)
XLA Ops:
  0.6 29.6 %coarse_blocks.1 = (f32[32,32]{1,0:T(8,128)S(1)}, f32[8,32,32]{2,1,0:T(8,128)S(1)}) custom-call(f32[3072,128]{1,0:T(8,128)} %bitcast.7, f32[96,32,128]{2,1,0:T(8,128)} %bitcast.8, s32[32,128]{1,0:T(8,128)} %bitcast.9, f32[8]{0:T(128)} %table.1, f32[432,192]{1,0:T(8,128)} %constant.2.clone.stencil), custom_call_target="tpu_custom_call" | custom-call | tf_op jit(solution)/shard_map/coarse_blocks/pallas_call | solution.py:465
  30.2 0.6 %copy.8 = f32[1,32,32]{2,1,0:T(8,128)} copy(f32[1,32,32]{2,1,0:T(8,128)S(1)} %bitcast.6) | data formatting | bytes 8192
  30.8 0.7 %copy.9 = f32[1,8,32,32]{3,2,1,0:T(8,128)} copy(f32[1,8,32,32]{3,2,1,0:T(8,128)S(1)} %bitcast.5) | data formatting | bytes 65536

commit v6 on v5

--- a/solution.py
+++ b/solution.py
@@ -174,11 +174,11 @@
     for p, r, copy in halo:
         pl.when(inside(p, r))(copy.start)
     faces = [
-        (1, 0, remote(planes.at[pl.ds(32 * a, 32), pl.ds(0, 8)], rx.at[pl.ds(32 * a, 32)], fs.at[a], fr.at[a], near(-1, 0), g))
-        for a in range(3)
+        (1, 0, remote(planes.at[pl.ds(16 * a, 16), pl.ds(0, 8)], rx.at[pl.ds(16 * a, 16)], fs.at[a], fr.at[a], near(-1, 0), g))
+        for a in range(6)
     ]
-    faces.append((0, 1, remote(fb, ry, fs.at[3], fr.at[3], near(0, -1), g)))
-    for p, r, copy in faces[3:] + faces[:1]:
+    faces.append((0, 1, remote(fb, ry, fs.at[6], fr.at[6], near(0, -1), g)))
+    for p, r, copy in faces[6:] + faces[:3]:
         pl.when(inside(-p, -r))(copy.start)
     lane24 = lax.broadcasted_iota(jnp.int32, (24, 128), 1)
 
@@ -212,7 +212,7 @@
         pl.semaphore_wait(hello.at[0], 1)
         to_high.start()
 
-    for p, r, copy in faces[1:3]:
+    for p, r, copy in faces[3:6]:
         pl.when(inside(-p, -r))(copy.start)
     load_c.wait()
     c_all[...] = c_in[...].astype(BF16)
@@ -374,7 +374,7 @@
 
     pl.semaphore_wait(ready, heard)
 
-    pl.when(inside(0, 1))(faces[3][2].wait_recv)
+    pl.when(inside(0, 1))(faces[6][2].wait_recv)
     block = scaled(dot_nt(qb[:, 24 * 128 : 36 * 128], split(jnp.concatenate([ry[t] for t in range(12)], axis=1))), inside(0, 1))
     inbox[g, 4] = pack(block)
     outbox[0] = pack(block.T)
@@ -388,7 +388,8 @@
     value_low = jnp.zeros((64, 64), F32)
     value_high = jnp.zeros((64, 64), F32)
     for a in range(3):
-        pl.when(inside(1, 0))(faces[a][2].wait_recv)
+        pl.when(inside(1, 0))(faces[2 * a][2].wait_recv)
+        pl.when(inside(1, 0))(faces[2 * a + 1][2].wait_recv)
         f = face(a)
         value = value + dot_nt(qb[:, a * 1024 : (a + 1) * 1024], f)
         value_low = value_low + dot_nt(side[0][:, 128 * a : 128 * a + 128], f[:, 0:128])
@@ -496,7 +497,7 @@
             pltpu.SMEM((8,), F32),
             pltpu.VMEM((3 * ROWS, 192), F32),
             pltpu.SemaphoreType.REGULAR((2,)), pltpu.SemaphoreType.REGULAR,
-            dma((4,)), dma((2,)), dma((2,)), dma((8,)), dma((8,)), dma((4,)), dma((4,)), dma((2,)), dma((2,)),
+            dma((4,)), dma((2,)), dma((2,)), dma((8,)), dma((8,)), dma((7,)), dma((7,)), dma((2,)), dma((2,)),
             dma((3,)), dma((3,)), dma((6, 4)), dma((6, 4)),
         ],
         compiler_params=pltpu.CompilerParams(

time: 32 us -> 31.7 us (level); the launches traced: 31.5 us -> 31.5 us
  no operation moved by 1% of the time
where the time goes in v6:
time: 31.7 us; the launch traced here: 31.5 us
  Pallas kernels  29.6 us (93%)
  local copies, waits for them, and re-layouts  1.26 us (4%)
  between operations  0.64 us (2%)
    pallas_call x1, Pallas kernels, shards(): pl.pallas_call(kernel, out_shape=(jax.ShapeDtypeStruct((32, 32), F32), ja...  29.6 us
    unnamed x2, local copies, waits for them, and re-layouts  1.26 us

profile of v6, /device:TPU:6, one launch (start us, length us, event | category | flops | bytes accessed | tf_op | source)
XLA Modules:
  0.0 31.5 jit_solution(16252756145662456428)
XLA Ops:
  0.6 29.6 %coarse_blocks.1 = (f32[32,32]{1,0:T(8,128)S(1)}, f32[8,32,32]{2,1,0:T(8,128)S(1)}) custom-call(f32[3072,128]{1,0:T(8,128)} %bitcast.7, f32[96,32,128]{2,1,0:T(8,128)} %bitcast.8, s32[32,128]{1,0:T(8,128)} %bitcast.9, f32[8]{0:T(128)} %table.1, f32[432,192]{1,0:T(8,128)} %constant.2.clone.stencil), custom_call_target="tpu_custom_call" | custom-call | tf_op jit(solution)/shard_map/coarse_blocks/pallas_call | solution.py:466
  30.3 0.6 %copy.8 = f32[1,32,32]{2,1,0:T(8,128)} copy(f32[1,32,32]{2,1,0:T(8,128)S(1)} %bitcast.6) | data formatting | bytes 8192
  30.9 0.7 %copy.9 = f32[1,8,32,32]{3,2,1,0:T(8,128)} copy(f32[1,8,32,32]{3,2,1,0:T(8,128)S(1)} %bitcast.5) | data formatting | bytes 65536

commit v7 on v6

--- a/solution.py
+++ b/solution.py
@@ -17,7 +17,7 @@
 GHOSTS = 42
 ROWS = 144
 ALL_NEAR = [(p, r) for p in (-1, 0, 1) for r in (-1, 0, 1) if (p, r) != (0, 0)]
-UNROLL_E = 8
+UNROLL_E = 32
 UNROLL_S = 2
 UNROLL_N = 2
 

time: 31.7 us -> 31.8 us (level)
  no operation moved by 1% of the time
where the time goes in v7:
time: 31.8 us; the launch traced here: 31.4 us
  Pallas kernels  29.5 us (93%)
  local copies, waits for them, and re-layouts  1.26 us (4%)
  between operations  0.64 us (2%)
    pallas_call x1, Pallas kernels, shards(): pl.pallas_call(kernel, out_shape=(jax.ShapeDtypeStruct((32, 32), F32), ja...  29.5 us
    unnamed x2, local copies, waits for them, and re-layouts  1.26 us

profile of v7, /device:TPU:6, one launch (start us, length us, event | category | flops | bytes accessed | tf_op | source)
XLA Modules:
  0.0 31.4 jit_solution(5190800472635960999)
XLA Ops:
  0.6 29.5 %coarse_blocks.1 = (f32[32,32]{1,0:T(8,128)S(1)}, f32[8,32,32]{2,1,0:T(8,128)S(1)}) custom-call(f32[3072,128]{1,0:T(8,128)} %bitcast.7, f32[96,32,128]{2,1,0:T(8,128)} %bitcast.8, s32[32,128]{1,0:T(8,128)} %bitcast.9, f32[8]{0:T(128)} %table.1, f32[432,192]{1,0:T(8,128)} %constant.2.clone.stencil), custom_call_target="tpu_custom_call" | custom-call | tf_op jit(solution)/shard_map/coarse_blocks/pallas_call | solution.py:466
  30.2 0.6 %copy.8 = f32[1,32,32]{2,1,0:T(8,128)} copy(f32[1,32,32]{2,1,0:T(8,128)S(1)} %bitcast.6) | data formatting | bytes 8192
  30.8 0.7 %copy.9 = f32[1,8,32,32]{3,2,1,0:T(8,128)} copy(f32[1,8,32,32]{3,2,1,0:T(8,128)S(1)} %bitcast.5) | data formatting | bytes 65536
